TPU v7x, 256 devices: a whole 4x4x8 slice. The times are simulated.
256 devices in a mesh: dp: 16 (over x_lo, y, core), space: 16 (over z, x_hi).
Axes of the slice: x: 4 (x_hi: 2, x_lo: 2; x = x_hi * 2 + x_lo), y: 4, z: 8, core: 2. Of those that a mesh axis runs over, the one named last changes fastest.
Arguments:
- features: bfloat16 [16, 32, 8, 8, 256], P('dp', 'space'), may hold values from -6 to 6
- weight_one: bfloat16 [27, 256, 256], P(None, 'dp'), may hold values from -0.078125 to 0.078125
- weight_two: bfloat16 [27, 256, 256], P(None, 'dp'), may hold values from -0.078125 to 0.078125
- cotangent: bfloat16 [16, 32, 8, 8, 256], P('dp', 'space'), may hold values from -6 to 6
Outputs:
- output: bfloat16 [16, 32, 8, 8, 256], P('dp', 'space')
- grad_input: bfloat16 [16, 32, 8, 8, 256], P('dp', 'space')
- grad_one: float32 [27, 256, 256], P(None, 'dp')
- grad_two: float32 [27, 256, 256], P(None, 'dp')
All inputs are finite; a program needn't handle non-finite values.
Results may differ from a plain program's by a relative error of at most 0.003.
Values may be sent and summed in bfloat16 or wider, within the bound.
A program may use at most 128 MiB of HBM per device.

v0:
```python
import jax
import jax.numpy as jnp
from jax import lax
from jax.sharding import PartitionSpec as P


def padded_2(cells, sides, width):
    for axis, dim in sides:
        count = lax.axis_size(axis)
        ends = count - 1
        head = lax.slice_in_dim(cells, 0, width, axis=dim)
        tail = lax.slice_in_dim(cells, cells.shape[dim] - width, cells.shape[dim], axis=dim)
        cells = jnp.concatenate(
            [
                lax.ppermute(tail, axis, [(i, (i + 1) % count) for i in range(ends)]),
                cells,
                lax.ppermute(head, axis, [((i + 1) % count, i) for i in range(ends)]),
            ],
            axis=dim,
        )
    return cells


def stencil_taps(padded, plane):
    depth_x = padded.shape[1] - 2
    depth_y = padded.shape[2] - 2
    depth_z = padded.shape[3] - 2
    chans = padded.shape[4]
    pieces = [
        padded[:, plane : plane + depth_x, j : j + depth_y, k : k + depth_z, :]
        for j in range(3)
        for k in range(3)
    ]
    return jnp.stack(pieces, axis=-2).reshape(-1, 9 * chans)


def convolve(padded, kernel):
    chans = padded.shape[4]
    total = jnp.zeros((1,), jnp.float32)
    for plane in range(3):
        block = kernel[9 * plane : 9 * plane + 9].reshape(9 * chans, -1)
        total = total + jnp.dot(
            stencil_taps(padded, plane), block, preferred_element_type=jnp.float32
        )
    return total


def weight_terms(padded, grad_out):
    chans = padded.shape[4]
    flat = grad_out.reshape(-1, grad_out.shape[-1])
    parts = [
        lax.dot_general(
            stencil_taps(padded, plane),
            flat,
            (((0,), (0,)), ((), ())),
            preferred_element_type=jnp.float32,
        )
        for plane in range(3)
    ]
    return jnp.concatenate(parts, axis=0).reshape(27, chans, flat.shape[1])


def flip_kernel(kernel):
    return jnp.flip(kernel, 0).transpose(0, 2, 1)


def pad_across(volume):
    return jnp.pad(volume, ((0, 0), (0, 0), (1, 1), (1, 1), (0, 0)))


def with_faces(volume):
    return padded_2(volume, (("space", 1),), 1)


def forward_rows(padded, shard):
    gathered = lax.all_gather(shard, "dp", axis=1, tiled=True)
    return convolve(padded, gathered)


def backward_rows(padded, shard):
    gathered = lax.all_gather(shard, "dp", axis=1, tiled=True)
    return convolve(padded, flip_kernel(gathered))


def shards(features, weight_one, weight_two, cotangent):
    shape = features.shape
    width = shape[4]
    count = shape[0] * lax.axis_size("dp") * shape[1] * lax.axis_size("space") * shape[2] * shape[3]
    factor = float(count) ** (-0.5)

    def kernel_grad(frame, grad_out):
        share = lax.psum_scatter(
            weight_terms(pad_across(frame), grad_out), "dp", scatter_dimension=1, tiled=True
        )
        return lax.psum(share, "space") * factor

    x_frame = with_faces(features)
    pre = forward_rows(pad_across(x_frame), weight_one)
    activated = jax.nn.silu(pre).astype(jnp.bfloat16).reshape(shape)
    act_frame = with_faces(activated)
    second = forward_rows(pad_across(act_frame), weight_two)
    output = (
        (features.reshape(-1, width).astype(jnp.float32) + second)
        .astype(jnp.bfloat16)
        .reshape(shape)
    )
    grad_frame = pad_across(with_faces(cotangent))
    grad_act = backward_rows(grad_frame, weight_two)
    sigmoid_val = jax.nn.sigmoid(pre)
    grad_pre = (
        (grad_act * sigmoid_val * (1.0 + pre * (1.0 - sigmoid_val)))
        .astype(jnp.bfloat16)
        .reshape(shape)
    )
    pre_frame = pad_across(with_faces(grad_pre))
    back_term = backward_rows(pre_frame, weight_one)
    grad_input = (
        (cotangent.reshape(-1, width).astype(jnp.float32) + back_term)
        .astype(jnp.bfloat16)
        .reshape(shape)
    )
    grad_two = kernel_grad(act_frame, cotangent)
    grad_one = kernel_grad(x_frame, grad_pre)
    return (output, grad_input, grad_one, grad_two)


def solution(mesh):
    in_specs = (
        P("dp", "space", None, None, None),
        P(None, "dp", None),
        P(None, "dp", None),
        P("dp", "space", None, None, None),
    )
    out_specs = (
        P("dp", "space", None, None, None),
        P("dp", "space", None, None, None),
        P(None, "dp", None),
        P(None, "dp", None),
    )
    return jax.shard_map(shards, mesh=mesh, in_specs=in_specs, out_specs=out_specs, check_vma=False)
```

profile of v0, /device:TPU:24, one launch (start us, length us, event | category | flops | bytes accessed | tf_op | source)
XLA Modules:
  0.0 426.5 jit_solution(15837241855566112461)
XLA Ops:
  10.0 6.1 %collective-permute-start = (bf16[1,1,8,8,256]{4,3,2,1,0:T(8,128)(2,1)S(1)}, bf16[1,1,8,8,256]{4,3,2,1,0:T(8,128)(2,1)S(1)}, u32[]{:S(2)}, u32[]{:S(2)}) collective-permute-start(bf16[1,1,8,8,256]{4,3,2,1,0:T(8,128)(2,1)S(1)} %get-tuple-element.92), channel_id=1, source_target_pairs={{0,1},{1,2},{2,3},{3,4},{4,5},{5,6},{6,7},{7,8},{8,9},{9,10},{10,1... | collective-permute-start | bytes 98312 | tf_op jit(solution)/shard_map/ppermute | solution.py:15
  18.2 6.5 %collective-permute-start.4 = (bf16[1,1,8,8,256]{4,3,2,1,0:T(8,128)(2,1)S(1)}, bf16[1,1,8,8,256]{4,3,2,1,0:T(8,128)(2,1)S(1)}, u32[]{:S(2)}, u32[]{:S(2)}) collective-permute-start(bf16[1,1,8,8,256]{4,3,2,1,0:T(8,128)(2,1)S(1)} %get-tuple-element.86), channel_id=1, source_target_pairs={{0,1},{1,2},{2,3},{3,4},{4,5},{5,6},{6,7},{7,8},{8,9},{9,10},{10,1... | collective-permute-start | bytes 98312 | tf_op jit(solution)/shard_map/ppermute | solution.py:15
  29.5 21.3 %all-gather.5.cloned.1.call-done = bf16[27,256,256]{2,1,0:T(8,128)(2,1)} async-done(((bf16[27,16,256]{2,1,0:T(8,128)(2,1)}), bf16[27,256,256]{2,1,0:T(8,128)(2,1)}) %all-gather.5.cloned.1.call-update) | async-done | bytes 3538960 | tf_op jit(solution)/shard_map/all_gather | solution.py:76
  50.9 2.4 reverse_bitcast_fusion.1
  54.5 2.4 copy.74
  57.0 1.6 copy.76
  58.5 1.5 copy.78
  60.0 31.4 %all-gather.3.cloned.1.call-done = bf16[27,256,256]{2,1,0:T(8,128)(2,1)} async-done(((bf16[27,16,256]{2,1,0:T(8,128)(2,1)}), bf16[27,256,256]{2,1,0:T(8,128)(2,1)}) %all-gather.3.cloned.1.call-update) | async-done | bytes 3538960 | tf_op jit(solution)/shard_map/all_gather | solution.py:76
  91.5 2.2 fusion.29
  100.2 3.2 pad_maximum_fusion
  104.8 6.1 %collective-permute-start.2 = (bf16[1,1,8,8,256]{4,3,2,1,0:T(8,128)(2,1)S(1)}, bf16[1,1,8,8,256]{4,3,2,1,0:T(8,128)(2,1)S(1)}, u32[]{:S(2)}, u32[]{:S(2)}) collective-permute-start(bf16[1,1,8,8,256]{4,3,2,1,0:T(8,128)(2,1)S(1)} %get-tuple-element.88), channel_id=1, source_target_pairs={{0,1},{1,2},{2,3},{3,4},{4,5},{5,6},{6,7},{7,8},{8,9},{9,10},{10,1... | collective-permute-start | bytes 98312 | tf_op jit(solution)/shard_map/ppermute | solution.py:15
  110.9 1.6 collective-permute-done.2
  114.9 3.3 pad_maximum_fusion.1
  118.3 1.6 fusion.30
  121.1 6.9 %collective-permute-start.6 = (bf16[1,1,8,8,256]{4,3,2,1,0:T(8,128)(2,1)}, bf16[1,1,8,8,256]{4,3,2,1,0:T(8,128)(2,1)}, u32[]{:S(2)}, u32[]{:S(2)}) collective-permute-start(bf16[1,1,8,8,256]{4,3,2,1,0:T(8,128)(2,1)} %get-tuple-element.82), channel_id=1, source_target_pairs={{0,1},{1,2},{2,3},{3,4},{4,5},{5,6},{6,7},{7,8},{8,9},{9,10},{10,1... | collective-permute-start | bytes 98312 | tf_op jit(solution)/shard_map/ppermute | solution.py:15
  128.3 1.9 fusion.26
  130.2 1.4 copy-done
  133.0 2.4 copy.87
  135.3 2.4 copy.89
  137.8 2.5 copy.91
  146.1 29.2 %reduce-scatter.3.cloned.1.call-done = f32[27,16,256]{2,1,0:T(8,128)} async-done(((f32[27,256,256]{2,1,0:T(8,128)}), f32[27,16,256]{2,1,0:T(8,128)}) %reduce-scatter.3.cloned.1.call-update) | async-done | bytes 442384 | tf_op jit(solution)/shard_map/reduce_scatter | solution.py:92
  175.3 76.1 %reduce-scatter.5.cloned.1.call-done = f32[27,16,256]{2,1,0:T(8,128)} async-done(((f32[27,256,256]{2,1,0:T(8,128)}), f32[27,16,256]{2,1,0:T(8,128)}) %reduce-scatter.5.cloned.1.call-update) | async-done | bytes 442384 | tf_op jit(solution)/shard_map/reduce_scatter | solution.py:92
  256.7 160.6 %all-reduce.7.cloned.1.call-done = (f32[27,16,256]{2,1,0:T(8,128)}, f32[27,16,256]{2,1,0:T(8,128)}) async-done(((f32[27,16,256]{2,1,0:T(8,128)}, f32[27,16,256]{2,1,0:T(8,128)}), (f32[27,16,256]{2,1,0:T(8,128)}, f32[27,16,256]{2,1,0:T(8,128)})) %all-reduce.7.cloned.1.call-update) | async-done | bytes 884752 | tf_op jit(solution)/shard_map/psum | solution.py:95
  417.3 1.9 broadcast_multiply_fusion.1
  (191 shorter events, 35.3 us)
Async XLA Ops:
  7.2 18.6 %copy-start.22 = (bf16[1,2,8,8,256]{4,3,2,1,0:T(8,128)(2,1)S(1)}, bf16[1,2,8,8,256]{4,3,2,1,0:T(8,128)(2,1)}, u32[]{:S(2)}) copy-start(bf16[1,2,8,8,256]{4,3,2,1,0:T(8,128)(2,1)} %param.4) | copy-start | bytes 196612
  7.2 43.7 %all-gather.5.cloned.1.call-start = ((), (), s32[]{:S(2)}) async-start(), calls=%async_computation.3 | async-start | bytes 3760128 | tf_op jit(solution)/shard_map/all_gather | solution.py:76
  7.9 83.6 %all-gather.3.cloned.1.call-start = ((), (), s32[]{:S(2)}) async-start(), calls=%async_computation.2 | async-start | bytes 3760128 | tf_op jit(solution)/shard_map/all_gather | solution.py:76
  8.7 16.0 %collective-permute-start.1 = (bf16[1,1,8,8,256]{4,3,2,1,0:T(8,128)(2,1)S(1)}, bf16[1,1,8,8,256]{4,3,2,1,0:T(8,128)(2,1)S(1)}, u32[]{:S(2)}, u32[]{:S(2)}) collective-permute-start(bf16[1,1,8,8,256]{4,3,2,1,0:T(8,128)(2,1)S(1)} %get-tuple-element.93), channel_id=1, source_target_pairs={{1,0},{2,1},{3,2},{4,3},{5,4},{6,5},{7,6},{8,7},{9,8},{10,9},{11,1... | collective-permute-start | bytes 98312 | tf_op jit(solution)/shard_map/ppermute | solution.py:17
  10.0 14.7 %collective-permute-start = (bf16[1,1,8,8,256]{4,3,2,1,0:T(8,128)(2,1)S(1)}, bf16[1,1,8,8,256]{4,3,2,1,0:T(8,128)(2,1)S(1)}, u32[]{:S(2)}, u32[]{:S(2)}) collective-permute-start(bf16[1,1,8,8,256]{4,3,2,1,0:T(8,128)(2,1)S(1)} %get-tuple-element.92), channel_id=1, source_target_pairs={{0,1},{1,2},{2,3},{3,4},{4,5},{5,6},{6,7},{7,8},{8,9},{9,10},{10,1... | collective-permute-start | bytes 98312 | tf_op jit(solution)/shard_map/ppermute | solution.py:15
  16.9 10.0 %collective-permute-start.5 = (bf16[1,1,8,8,256]{4,3,2,1,0:T(8,128)(2,1)S(1)}, bf16[1,1,8,8,256]{4,3,2,1,0:T(8,128)(2,1)S(1)}, u32[]{:S(2)}, u32[]{:S(2)}) collective-permute-start(bf16[1,1,8,8,256]{4,3,2,1,0:T(8,128)(2,1)S(1)} %get-tuple-element.87), channel_id=1, source_target_pairs={{1,0},{2,1},{3,2},{4,3},{5,4},{6,5},{7,6},{8,7},{9,8},{10,9},{11,1... | collective-permute-start | bytes 98312 | tf_op jit(solution)/shard_map/ppermute | solution.py:17
  18.2 8.8 %collective-permute-start.4 = (bf16[1,1,8,8,256]{4,3,2,1,0:T(8,128)(2,1)S(1)}, bf16[1,1,8,8,256]{4,3,2,1,0:T(8,128)(2,1)S(1)}, u32[]{:S(2)}, u32[]{:S(2)}) collective-permute-start(bf16[1,1,8,8,256]{4,3,2,1,0:T(8,128)(2,1)S(1)} %get-tuple-element.86), channel_id=1, source_target_pairs={{0,1},{1,2},{2,3},{3,4},{4,5},{5,6},{6,7},{7,8},{8,9},{9,10},{10,1... | collective-permute-start | bytes 98312 | tf_op jit(solution)/shard_map/ppermute | solution.py:15
  24.7 150.7 %reduce-scatter.3.cloned.1.call-start = ((), (), s32[]{:S(2)}) async-start(), calls=%async_computation.4 | async-start | bytes 7520256 | tf_op jit(solution)/shard_map/reduce_scatter | solution.py:92
  29.4 21.5 %copy-start.16 = (bf16[1,2,8,8,9,256]{5,3,4,2,1,0:T(8,128)(2,1)}, bf16[1,2,8,8,9,256]{5,3,4,2,1,0:T(8,128)(2,1)S(1)}, u32[]{:S(2)}) copy-start(bf16[1,2,8,8,9,256]{5,3,4,2,1,0:T(8,128)(2,1)S(1)} %constant_dynamic-update-slice_fusion) | copy-start | bytes 1769476
  29.5 21.3 %copy-start.26 = (bf16[1,2,8,8,9,256]{5,3,4,2,1,0:T(8,128)(2,1)}, bf16[1,2,8,8,9,256]{5,3,4,2,1,0:T(8,128)(2,1)S(1)}, u32[]{:S(2)}) copy-start(bf16[1,2,8,8,9,256]{5,3,4,2,1,0:T(8,128)(2,1)S(1)} %constant_dynamic-update-slice_fusion.54) | copy-start | bytes 1769476
  60.0 33.7 %copy-start.17 = (bf16[1,2,8,8,9,256]{5,3,4,2,1,0:T(8,128)(2,1)S(1)}, bf16[1,2,8,8,9,256]{5,3,4,2,1,0:T(8,128)(2,1)}, u32[]{:S(2)}) copy-start(bf16[1,2,8,8,9,256]{5,3,4,2,1,0:T(8,128)(2,1)} %copy-done.16) | copy-start | bytes 1769476
  103.4 148.0 %reduce-scatter.5.cloned.1.call-start = ((), (), s32[]{:S(2)}) async-start(), calls=%async_computation.5 | async-start | bytes 7520256 | tf_op jit(solution)/shard_map/reduce_scatter | solution.py:92
  103.5 7.4 %collective-permute-start.3 = (bf16[1,1,8,8,256]{4,3,2,1,0:T(8,128)(2,1)S(1)}, bf16[1,1,8,8,256]{4,3,2,1,0:T(8,128)(2,1)S(1)}, u32[]{:S(2)}, u32[]{:S(2)}) collective-permute-start(bf16[1,1,8,8,256]{4,3,2,1,0:T(8,128)(2,1)S(1)} %get-tuple-element.89), channel_id=1, source_target_pairs={{1,0},{2,1},{3,2},{4,3},{5,4},{6,5},{7,6},{8,7},{9,8},{10,9},{11,1... | collective-permute-start | bytes 98312 | tf_op jit(solution)/shard_map/ppermute | solution.py:17
  104.8 7.6 %collective-permute-start.2 = (bf16[1,1,8,8,256]{4,3,2,1,0:T(8,128)(2,1)S(1)}, bf16[1,1,8,8,256]{4,3,2,1,0:T(8,128)(2,1)S(1)}, u32[]{:S(2)}, u32[]{:S(2)}) collective-permute-start(bf16[1,1,8,8,256]{4,3,2,1,0:T(8,128)(2,1)S(1)} %get-tuple-element.88), channel_id=1, source_target_pairs={{0,1},{1,2},{2,3},{3,4},{4,5},{5,6},{6,7},{7,8},{8,9},{9,10},{10,1... | collective-permute-start | bytes 98312 | tf_op jit(solution)/shard_map/ppermute | solution.py:15
  118.2 9.8 %copy-start.1 = (bf16[27,256,256]{2,1,0:T(8,128)(2,1)S(1)}, bf16[27,256,256]{2,1,0:T(8,128)(2,1)}, u32[]{:S(2)}) copy-start(bf16[27,256,256]{2,1,0:T(8,128)(2,1)} %all-gather.3.cloned.1.call-done) | copy-start | bytes 10616836
  118.2 299.1 %all-reduce.7.cloned.1.call-start = ((), (), s32[]{:S(2)}) async-start(), calls=%async_computation.6 | async-start | bytes 1769472 | tf_op jit(solution)/shard_map/psum | solution.py:95
  119.8 20.4 %collective-permute-start.7 = (bf16[1,1,8,8,256]{4,3,2,1,0:T(8,128)(2,1)}, bf16[1,1,8,8,256]{4,3,2,1,0:T(8,128)(2,1)}, u32[]{:S(2)}, u32[]{:S(2)}) collective-permute-start(bf16[1,1,8,8,256]{4,3,2,1,0:T(8,128)(2,1)} %get-tuple-element.83), channel_id=1, source_target_pairs={{1,0},{2,1},{3,2},{4,3},{5,4},{6,5},{7,6},{8,7},{9,8},{10,9},{11,1... | collective-permute-start | bytes 98312 | tf_op jit(solution)/shard_map/ppermute | solution.py:17
  121.1 19.1 %collective-permute-start.6 = (bf16[1,1,8,8,256]{4,3,2,1,0:T(8,128)(2,1)}, bf16[1,1,8,8,256]{4,3,2,1,0:T(8,128)(2,1)}, u32[]{:S(2)}, u32[]{:S(2)}) collective-permute-start(bf16[1,1,8,8,256]{4,3,2,1,0:T(8,128)(2,1)} %get-tuple-element.82), channel_id=1, source_target_pairs={{0,1},{1,2},{2,3},{3,4},{4,5},{5,6},{6,7},{7,8},{8,9},{9,10},{10,1... | collective-permute-start | bytes 98312 | tf_op jit(solution)/shard_map/ppermute | solution.py:15
  128.3 3.3 copy-start
  137.8 2.5 copy-start.15
  142.0 2.1 copy-start.6
  142.0 2.1 copy-start.19
  143.2 1.6 copy-start.10
  417.3 1.9 copy-start.30
  (20 other events, 24.4 us)
Sparse Core Ops, SparseCore 0:
  9.8 41.0 all-gather.4
  52.7 38.7 all-gather.2
  103.6 71.7 reduce-scatter.2
  177.9 73.4 reduce-scatter.4
  254.0 163.2 all-reduce.6
where the time goes:
time: 428 us; the launch traced here: 427 us
  waiting for transfers between devices  321 us (75%)
  local copies, waits for them, and re-layouts  38.1 us (9%)
  starting transfers between devices  30.8 us (7%)
  between operations  14.8 us (3%)
  other arithmetic  12.9 us (3%)
  matrix products  8.85 us (2%)
    psum x1, waiting for transfers between devices, kernel_grad(): return lax.psum(share, 'space') * factor  161 us
    reduce_scatter x2, waiting for transfers between devices, kernel_grad(): lax.psum_scatter(weight_terms(pad_across(frame), grad_out), 'dp', scatter...  105 us
    all_gather x2, waiting for transfers between devices, forward_rows(): gathered = lax.all_gather(shard, 'dp', axis=1, tiled=True)  52.8 us
    ppermute x4, starting transfers between devices, padded_2(): lax.ppermute(tail, axis, [(i, (i + 1) % count) for i in range(ends)])  25.5 us
    slice x10, local copies, waits for them, and re-layouts, convolve(): block = kernel[9 * plane:9 * plane + 9].reshape(9 * chans, -1)  19.5 us
  transfers between devices with their start and end apart: 13, of which 6 were waited for; matrix products, arithmetic and copies ran while one was open for 10% of the time, Pallas kernels for 0%

commit v1 on v0

v1 whole, which is shorter than its diff:
```python
import functools

import jax
import jax.numpy as jnp
from jax import lax
from jax.experimental import pallas as pl
from jax.experimental.pallas import tpu as pltpu
from jax.sharding import PartitionSpec as P

MESH = pl.DeviceIdType.MESH
F32 = jnp.float32
BF16 = jnp.bfloat16
C = 256
TAPS = 27
ROWS = TAPS * 16


def dot(a, b, dims=((1,), (0,))):
    return lax.dot_general(a, b, (dims, ((), ())), preferred_element_type=F32)


def lanes():
    return lax.broadcasted_iota(jnp.int32, (16, 128), 1)


def lower():
    return lanes() % 128 < 64


def half_turn(v):
    return pltpu.roll(v, 64, 1)


def inside(j, k, sign):
    lane = lanes()
    y = (lane // 8) % 8 + sign * (j - 1)
    z = lane % 8 + sign * (k - 1)
    return (y >= 0) & (y < 8) & (z >= 0) & (z < 8)


def shifted(v, j, k, sign):
    delta = sign * (8 * (j - 1) + (k - 1))
    if delta == 0:
        return v
    parts = v.shape[0] // 16
    keep = inside(j, k, sign)
    if parts > 1:
        keep = jnp.concatenate([keep] * parts, axis=0)
    return jnp.where(keep, pltpu.roll(v, (-delta) % 128, 1), 0.0)


def regroup(w_ref, z_ref):
    group = lanes() // 16
    for q in range(4):
        for h in range(2):
            tiles = []
            for i in range(8):
                tap = 8 * q + i
                if tap < TAPS:
                    tiles.append(w_ref[16 * tap : 16 * tap + 16, 128 * h : 128 * h + 128].astype(F32))
                else:
                    tiles.append(jnp.zeros((16, 128), F32))
            for bit in (1, 2, 4):
                low = (group & bit) == 0
                for i in range(8):
                    if i & bit:
                        continue
                    a, b = tiles[i], tiles[i + bit]
                    tiles[i] = jnp.where(low, a, pltpu.roll(b, 16 * bit, 1))
                    tiles[i + bit] = jnp.where(low, pltpu.roll(a, 128 - 16 * bit, 1), b)
            for i in range(8):
                z_ref[8 * h + i, :, 128 * q : 128 * q + 128] = tiles[i].astype(BF16)


def gather_taps(y_ref, p_ref, hm_ref, hp_ref, tensor, chip, sign):
    lo = lower()
    lefts = []
    for half in range(2):
        at = slice(128 * half, 128 * half + 128)
        total = None
        for j in range(3):
            for k in range(3):
                rows = [16 * (9 * i + 3 * j + k) for i in range(3)]
                first, mid, last = [y_ref[r : r + 16, at] for r in rows]
                if sign < 0:
                    first, last = last, first
                inner = jnp.where(lo, first, last)
                outer = jnp.where(lo, last, first)
                term = shifted(jnp.concatenate([mid, inner, outer], axis=0), j, k, sign)
                total = term if total is None else total + term
        p_ref[tensor, chip, :, at] = total[:16] + half_turn(total[16:32])
        lefts.append(total[32:])
    hm_ref[tensor, chip] = jnp.where(lo, lefts[0], half_turn(lefts[1]))
    hp_ref[tensor, chip] = jnp.where(lo, half_turn(lefts[0]), lefts[1])


def spread_halo(hp, hm, first, final):
    lo = lower()
    hp = jnp.where(first, 0.0, hp)
    hm = jnp.where(final, 0.0, hm)
    return [jnp.where(lo, hp, half_turn(hm)), jnp.where(lo, half_turn(hp), hm)]


def edge_planes(v):
    lo = lower()
    a, b = v[:, :128], v[:, 128:]
    return jnp.where(lo, a, half_turn(b)), jnp.where(lo, half_turn(a), b)


def scatter_taps(v, halos, im_ref, chip):
    lo = lower()
    for half in range(2):
        at = slice(128 * half, 128 * half + 128)
        own = v[:, at]
        turned = half_turn(own)
        stack = jnp.concatenate(
            [jnp.where(lo, halos[half], turned), own, jnp.where(lo, turned, halos[half])], axis=0
        )
        for j in range(3):
            for k in range(3):
                term = shifted(stack, j, k, 1).astype(BF16)
                for i in range(3):
                    row = 16 * (9 * i + 3 * j + k)
                    im_ref[chip, row : row + 16, at] = term[16 * i : 16 * i + 16]


def kernel(
    factor,
    x_ref, g_ref, w1_ref, w2_ref,
    out_ref, gin_ref, one_ref, two_ref,
    ga, gb, z1, z2, r1, r2, f1, f2, y_ref, p_ref, hm, hp, rhm, rhp,
    xm, xp, rxm, rxp, am, ap, ram, rap, imx, ima, gsum, gb16, rr, full, oc, oall,
    w_send, w_recv, a_send, a_recv, s_send, s_recv, b_send, b_recv, t_send, t_recv,
    n_send, n_recv, r_send, r_recv, f_send, f_recv, o_send, o_recv,
):
    d = lax.axis_index("dp")
    s = lax.axis_index("space")
    m = d // 2
    e = d - 2 * m
    above = lax.rem(s + 1, 16)
    below = lax.rem(s + 15, 16)
    first, final = s == 0, s == 15
    sibling = 2 * m + 1 - e
    core_at = pl.ds(pl.multiple_of(e * 128, 128), 128)
    core_other = pl.ds(pl.multiple_of((1 - e) * 128, 128), 128)
    own_rows = pl.ds(pl.multiple_of(d * 16, 16), 16)

    def rows_of(index, count):
        return pl.ds(pl.multiple_of(index * count, count), count)

    def remote(src, dst, send, recv, dp, space):
        return pltpu.make_async_remote_copy(
            src_ref=src, dst_ref=dst, send_sem=send, recv_sem=recv, device_id=(dp, space), device_id_type=MESH
        )

    def each(count, body, start=0):
        def step(i, carry):
            body(i)
            return carry

        lax.fori_loop(start, count, step, 0)

    barrier = pltpu.get_barrier_semaphore()

    def greet(r):
        pl.semaphore_signal(barrier, inc=1, device_id=(lax.rem(d + r, 16), s), device_id_type=MESH)
        pl.semaphore_signal(barrier, inc=1, device_id=(d, lax.rem(s + r, 16)), device_id_type=MESH)

    each(16, greet, 1)

    ga[m, 0, :, core_at] = x_ref[...].astype(F32).T.astype(BF16)
    ga[m, 1, :, core_at] = g_ref[...].astype(F32).T.astype(BF16)
    regroup(w1_ref, z1)
    regroup(w2_ref, z2)
    gb16[:, ROWS:, :] = jnp.zeros((2, 80, C), BF16)
    pl.semaphore_wait(barrier, 30)

    def send_slices(which, z, r):
        def body(step):
            to = lax.rem(d + step, 16)
            remote(z.at[to], r.at[own_rows], w_send.at[which, to], w_recv.at[which, d], to, s).start()

        each(16, body, 1)
        r[own_rows] = z[d]

    def wait_slices(which, z, r):
        def body(step):
            at = lax.rem(d + 16 - step, 16)
            copy = remote(z.at[at], r.at[rows_of(at, 16)], w_send.at[which, at], w_recv.at[which, at], at, s)
            copy.wait_recv()
            copy.wait_send()

        each(16, body, 1)

    def block_a(chip, where):
        return ga.at[chip, :, :, where]

    def across_a(step, chip):
        to = lax.rem(m + step, 8)
        return remote(block_a(chip, core_at), block_a(chip, core_at), a_send.at[step], a_recv.at[chip], 2 * to + e, s)

    def beside_a(chip, where):
        return remote(block_a(chip, where), block_a(chip, where), s_send.at[chip], s_recv.at[chip], sibling, s)

    send_slices(0, z1, r1)
    beside_a(m, core_at).start()
    each(8, lambda step: across_a(step, m).start(), 1)
    send_slices(1, z2, r2)
    wait_slices(0, z1, r1)
    f1[...] = r1[...].astype(F32).T.astype(BF16)

    def phase_one(step):
        @pl.when(step < 8)
        def _():
            chip = lax.rem(m + 8 - step, 8)
            across_a(step, chip).wait_recv()
            beside_a(chip, core_at).start()

        chip = lax.rem(m + 9 - step, 8)
        beside_a(chip, core_other).wait_recv()
        y_ref[...] = dot(f1[:ROWS], ga[chip, 0])
        gather_taps(y_ref, p_ref, hm.at[0], hp.at[0], 0, chip, 1)
        y_ref[...] = dot(w2_ref[...], ga[chip, 1])
        gather_taps(y_ref, p_ref, hm.at[0], hp.at[0], 1, chip, -1)

    each(9, phase_one, 1)

    def near(index, src, dst, to):
        return remote(src, dst, n_send.at[index], n_recv.at[index], d, to)

    near(0, hm.at[0], rhm.at[0], below).start()
    near(1, hp.at[0], rhp.at[0], above).start()

    def x_edges(chip):
        v = ga[chip, 0, own_rows, :].astype(F32)
        lowest, highest = edge_planes(v)
        xm[chip] = lowest.astype(BF16)
        xp[chip] = highest.astype(BF16)

    each(8, x_edges)
    near(2, xm, rxm, below).start()
    near(3, xp, rxp, above).start()

    near(0, hm.at[0], rhm.at[0], below).wait_recv()
    near(1, hp.at[0], rhp.at[0], above).wait_recv()

    def middle(chip):
        halo = [spread_halo(rhp[0, t, chip], rhm[0, t, chip], first, final) for t in range(2)]
        pre = p_ref[0, chip] + jnp.concatenate(halo[0], axis=1)
        grad = p_ref[1, chip] + jnp.concatenate(halo[1], axis=1)
        sig = jax.nn.sigmoid(pre)
        act = (pre * sig).astype(BF16)
        gb[0, chip, own_rows, :] = act
        gb[1, chip, own_rows, :] = (grad * sig * (1.0 + pre * (1.0 - sig))).astype(BF16)
        lowest, highest = edge_planes(act.astype(F32))
        am[chip] = lowest.astype(BF16)
        ap[chip] = highest.astype(BF16)

    each(8, middle)

    def block_b(tensor, owner):
        return gb.at[tensor, :, rows_of(owner, 16), :]

    def across_b(tensor, step, owner):
        to = 2 * lax.rem(m + step, 8) + e
        return remote(
            block_b(tensor, owner), block_b(tensor, owner),
            b_send.at[tensor, step], b_recv.at[tensor, owner // 2], to, s,
        )

    def beside_b(tensor, owner):
        return remote(
            block_b(tensor, owner), block_b(tensor, owner),
            t_send.at[tensor, owner // 2], t_recv.at[tensor, owner // 2], sibling, s,
        )

    near(4, am, ram, below).start()
    near(5, ap, rap, above).start()
    for tensor in (1, 0):
        beside_b(tensor, d).start()
        each(8, lambda step: across_b(tensor, step, d).start(), 1)

    near(2, xm, rxm, below).wait_recv()
    near(3, xp, rxp, above).wait_recv()

    def taps_x(chip):
        halos = spread_halo(rxp[chip].astype(F32), rxm[chip].astype(F32), first, final)
        scatter_taps(ga[chip, 0, own_rows, :].astype(F32), halos, imx, chip)

    each(8, taps_x)

    near(4, am, ram, below).wait_recv()
    near(5, ap, rap, above).wait_recv()

    def taps_a(chip):
        halos = spread_halo(rap[chip].astype(F32), ram[chip].astype(F32), first, final)
        scatter_taps(gb[0, chip, own_rows, :].astype(F32), halos, ima, chip)

    each(8, taps_a)

    def reduce_copy(which, to, source):
        return remote(
            gb16.at[which, rows_of(to, 32)], rr.at[which, source],
            r_send.at[which, to], r_recv.at[which, source], d, to,
        )

    def send_partial(which, im, operand):
        gsum[...] = dot(im[0], operand(0), ((1,), (1,)))

        def add(chip):
            gsum[...] += dot(im[chip], operand(chip), ((1,), (1,)))

        each(8, add, 1)
        gb16[which, :ROWS] = gsum[...].astype(BF16)
        each(16, lambda step: reduce_copy(which, lax.rem(s + step, 16), s).start(), 1)
        rr[which, s] = gb16[which, rows_of(s, 32)]

    def spread_copy(which, to, owner):
        block = full.at[which, rows_of(owner, 32)]
        return remote(block, block, f_send.at[which, to], f_recv.at[which, owner], d, to)

    def reduce(which):
        def body(step):
            source = lax.rem(s + 16 - step, 16)
            reduce_copy(which, source, source).wait_recv()

        each(16, body, 1)
        total = rr[which, 0].astype(F32)
        for source in range(1, 16):
            total += rr[which, source].astype(F32)
        full[which, rows_of(s, 32)] = total * factor
        each(16, lambda step: spread_copy(which, lax.rem(s + step, 16), s).start(), 1)

    send_partial(1, ima, lambda chip: ga[chip, 1])

    def arrive_b(tensor):
        def forward(step):
            owner = 2 * lax.rem(m + 8 - step, 8) + e
            across_b(tensor, step, owner).wait_recv()
            beside_b(tensor, owner).start()

        each(8, forward, 1)
        each(8, lambda chip: beside_b(tensor, 2 * chip + 1 - e).wait_recv())

    arrive_b(1)
    send_partial(0, imx, lambda chip: gb[1, chip])
    arrive_b(0)
    wait_slices(1, z2, r2)
    f2[...] = r2[...].astype(F32).T.astype(BF16)
    reduce(1)

    def phase_two(chip):
        y_ref[...] = dot(f2[:ROWS], gb[0, chip])
        gather_taps(y_ref, p_ref, hm.at[1], hp.at[1], 0, chip, 1)
        y_ref[...] = dot(w1_ref[...], gb[1, chip])
        gather_taps(y_ref, p_ref, hm.at[1], hp.at[1], 1, chip, -1)

    each(8, phase_two)
    near(6, hm.at[1], rhm.at[1], below).start()
    near(7, hp.at[1], rhp.at[1], above).start()
    reduce(0)
    near(6, hm.at[1], rhm.at[1], below).wait_recv()
    near(7, hp.at[1], rhp.at[1], above).wait_recv()

    def finish(chip):
        for t in range(2):
            halo = spread_halo(rhp[1, t, chip], rhm[1, t, chip], first, final)
            total = p_ref[t, chip] + jnp.concatenate(halo, axis=1)
            total = (ga[chip, t, own_rows, :].astype(F32) + total).astype(BF16)
            oc[t, 2 * chip] = total[:, :128]
            oc[t, 2 * chip + 1] = total[:, 128:]

    each(8, finish)

    def home(t, to, source):
        return remote(
            oc.at[t, to], oall.at[t, rows_of(source, 16)], o_send.at[t, to], o_recv.at[t, source], to, s
        )

    def send_home(step):
        for t in range(2):
            home(t, lax.rem(d + step, 16), d).start()

    each(16, send_home, 1)
    for t in range(2):
        oall[t, own_rows] = oc[t, d]

    def wait_home(step):
        for t in range(2):
            source = lax.rem(d + 16 - step, 16)
            home(t, source, source).wait_recv()

    each(16, wait_home, 1)
    out_ref[...] = oall[0].astype(F32).T.astype(BF16)
    gin_ref[...] = oall[1].astype(F32).T.astype(BF16)

    def wait_spread(step):
        for which in range(2):
            owner = lax.rem(s + 16 - step, 16)
            spread_copy(which, owner, owner).wait_recv()

    each(16, wait_spread, 1)
    one_ref[...] = full[0, :ROWS]
    two_ref[...] = full[1, :ROWS]

    def wait_far(step):
        to = lax.rem(s + step, 16)
        for which in range(2):
            reduce_copy(which, to, s).wait_send()
            spread_copy(which, to, s).wait_send()
            home(which, lax.rem(d + step, 16), d).wait_send()

    each(16, wait_far, 1)

    def wait_across(step):
        across_a(step, m).wait_send()
        for tensor in range(2):
            across_b(tensor, step, d).wait_send()

    each(8, wait_across, 1)

    def wait_beside(chip):
        beside_a(chip, core_at).wait_send()
        for tensor in range(2):
            beside_b(tensor, 2 * chip + e).wait_send()

    each(8, wait_beside)
    near(0, hm.at[0], rhm.at[0], below).wait_send()
    near(1, hp.at[0], rhp.at[0], above).wait_send()
    near(2, xm, rxm, below).wait_send()
    near(3, xp, rxp, above).wait_send()
    near(4, am, ram, below).wait_send()
    near(5, ap, rap, above).wait_send()
    near(6, hm.at[1], rhm.at[1], below).wait_send()
    near(7, hp.at[1], rhp.at[1], above).wait_send()


def shards(features, weight_one, weight_two, cotangent):
    shape = features.shape
    count = shape[0] * lax.axis_size("dp") * shape[1] * lax.axis_size("space") * shape[2] * shape[3]
    factor = float(count) ** (-0.5)
    vmem = pl.BlockSpec(memory_space=pltpu.VMEM)
    dma = pltpu.SemaphoreType.DMA
    halo = lambda dtype, *lead: pltpu.VMEM((*lead, 8, 16, 128), dtype)
    out, gin, one, two = pl.pallas_call(
        functools.partial(kernel, factor),
        out_shape=[
            jax.ShapeDtypeStruct((128, C), BF16),
            jax.ShapeDtypeStruct((128, C), BF16),
            jax.ShapeDtypeStruct((ROWS, C), F32),
            jax.ShapeDtypeStruct((ROWS, C), F32),
        ],
        in_specs=[vmem] * 4,
        out_specs=[vmem] * 4,
        scratch_shapes=[
            pltpu.VMEM((8, 2, C, C), BF16),
            pltpu.VMEM((2, 8, C, C), BF16),
            pltpu.VMEM((16, 16, 512), BF16),
            pltpu.VMEM((16, 16, 512), BF16),
            pltpu.VMEM((C, 512), BF16),
            pltpu.VMEM((C, 512), BF16),
            pltpu.VMEM((512, C), BF16),
            pltpu.VMEM((512, C), BF16),
            pltpu.VMEM((ROWS, C), F32),
            pltpu.VMEM((2, 8, 16, C), F32),
            halo(F32, 2, 2), halo(F32, 2, 2), halo(F32, 2, 2), halo(F32, 2, 2),
            halo(BF16), halo(BF16), halo(BF16), halo(BF16),
            halo(BF16), halo(BF16), halo(BF16), halo(BF16),
            pltpu.VMEM((8, ROWS, C), BF16),
            pltpu.VMEM((8, ROWS, C), BF16),
            pltpu.VMEM((ROWS, C), F32),
            pltpu.VMEM((2, 512, C), BF16),
            pltpu.VMEM((2, 16, 32, C), BF16),
            pltpu.VMEM((2, 512, C), F32),
            pltpu.VMEM((2, 16, 16, 128), BF16),
            pltpu.VMEM((2, C, 128), BF16),
            dma((2, 16)), dma((2, 16)),
            dma((8,)), dma((8,)), dma((8,)), dma((8,)),
            dma((2, 8)), dma((2, 8)), dma((2, 8)), dma((2, 8)),
            dma((8,)), dma((8,)),
            dma((2, 16)), dma((2, 16)), dma((2, 16)), dma((2, 16)), dma((2, 16)), dma((2, 16)),
        ],
        compiler_params=pltpu.CompilerParams(
            collective_id=0, has_side_effects=True, vmem_limit_bytes=40 * 2**20
        ),
    )(
        features.reshape(128, C), cotangent.reshape(128, C),
        weight_one.reshape(ROWS, C), weight_two.reshape(ROWS, C),
    )
    return out.reshape(shape), gin.reshape(shape), one.reshape(TAPS, 16, C), two.reshape(TAPS, 16, C)


def solution(mesh):
    in_specs = (
        P("dp", "space", None, None, None),
        P(None, "dp", None),
        P(None, "dp", None),
        P("dp", "space", None, None, None),
    )
    out_specs = (
        P("dp", "space", None, None, None),
        P("dp", "space", None, None, None),
        P(None, "dp", None),
        P(None, "dp", None),
    )
    return jax.shard_map(shards, mesh=mesh, in_specs=in_specs, out_specs=out_specs, check_vma=False)
```

time: 428 us -> 103 us (0.24)
  waiting for transfers between devices: 321 us -> 0 us
  Pallas kernels: 0 us -> 93.6 us
  local copies, waits for them, and re-layouts: 38.1 us -> 6.33 us
  starting transfers between devices: 30.8 us -> 0 us
  between operations: 14.8 us -> 0.65 us
  other arithmetic: 12.9 us -> 0 us
  matrix products: 8.85 us -> 0 us
    psum x1 -> x0, waiting for transfers between devices: 161 us -> none  [kernel_grad(): return lax.psum(share, 'space') * factor]
    reduce_scatter x2 -> x0, waiting for transfers between devices: 105 us -> none  [kernel_grad(): lax.psum_scatter(weight_terms(pad_across(frame), grad_out), 'dp', scatter...]
    pallas_call x0 -> x1, Pallas kernels: none -> 93.6 us  [shards(): pl.pallas_call(functools.partial(kernel, factor), out_shape=[jax.ShapeDty...]
    all_gather x2 -> x0, waiting for transfers between devices: 52.8 us -> none  [forward_rows(): gathered = lax.all_gather(shard, 'dp', axis=1, tiled=True)]
    ppermute x8 -> x0, starting transfers between devices: 30.6 us -> none  [the longest x4 25.5 us: padded_2(): lax.ppermute(tail, axis, [(i, (i + 1) % count) for i in range(ends)])]
    slice x14 -> x0, local copies, waits for them, and re-layouts: 22.7 us -> none  [the longest x10 19.5 us: convolve(): block = kernel[9 * plane:9 * plane + 9].reshape(9 * chans, -1)]
    dot_general x18 -> x0, matrix products: 8.85 us -> none  [the longest x12 5.89 us: convolve(): jnp.dot(stencil_taps(padded, plane), block, preferred_element_type=jnp.fl...]
    concatenate x6 -> x0, other arithmetic: 8.49 us -> none  [the longest x2 6.42 us: weight_terms(): return jnp.concatenate(parts, axis=0).reshape(27, chans, flat.shape[1])]
  transfers between devices with their start and end apart: 13 -> 0, of which waited for: 6 -> 0; matrix products, arithmetic and copies ran while one was open for 10% -> 0% of each run, Pallas kernels for 0% -> 0%
where the time goes in v1:
time: 103 us; the launch traced here: 101 us
  Pallas kernels  93.6 us (91%)
  local copies, waits for them, and re-layouts  6.33 us (6%)
    pallas_call x1, Pallas kernels, shards(): pl.pallas_call(functools.partial(kernel, factor), out_shape=[jax.ShapeDty...  93.6 us
    unnamed x12, local copies, waits for them, and re-layouts  6.33 us

profile of v1, /device:TPU:24, one launch (start us, length us, event | category | flops | bytes accessed | tf_op | source)
XLA Modules:
  0.0 100.6 jit_solution(2090818545347305192)
XLA Ops:
  0.6 0.0 copy-start
  0.6 0.9 copy-done
  1.6 0.0 copy-start.1
  1.6 0.9 copy-done.1
  2.5 0.0 copy-start.2
  2.5 0.8 copy-done.2
  3.3 0.0 copy-start.3
  3.3 0.8 copy-done.3
  4.2 93.6 %shard_map.75 = (bf16[128,256]{1,0:T(8,128)(2,1)S(1)}, bf16[128,256]{1,0:T(8,128)(2,1)S(1)}, f32[432,256]{1,0:T(8,128)S(1)}, f32[432,256]{1,0:T(8,128)S(1)}) custom-call(bf16[128,256]{1,0:T(8,128)(2,1)S(1)} %bitcast.12, bf16[128,256]{1,0:T(8,128)(2,1)S(1)} %bitcast.13, bf16[432,256]{1,0:T(8,128)(2,1)S(1)} %bitcast.10, bf16[432,256]{1,0:T(8,128)(2,1)S(1)} %bitcast.11), custom_call_target="tpu_custom_call" | custom-call | tf_op jit(solution)/shard_map/pallas_call | solution.py:445
  97.8 0.6 copy.12
  98.5 0.6 copy.13
  99.1 0.8 copy.14
  99.9 0.8 copy.15
Async XLA Ops:
  0.6 0.9 copy-start
  1.6 0.9 copy-start.1
  2.5 0.8 copy-start.2
  3.3 0.8 copy-start.3

commit v2 on v0

v2 whole, which is shorter than its diff:
```python
import functools

import jax
import jax.numpy as jnp
from jax import lax
from jax.experimental import pallas as pl
from jax.experimental.pallas import tpu as pltpu
from jax.sharding import PartitionSpec as P

MESH = pl.DeviceIdType.MESH
F32 = jnp.float32
BF16 = jnp.bfloat16
C = 256
TAPS = 27
ROWS = TAPS * 16
TILES = 2 * TAPS
SHARE = -(-TILES // 8)


def dot(a, b, dims=((1,), (0,))):
    return lax.dot_general(a, b, (dims, ((), ())), preferred_element_type=F32)


def lanes():
    return lax.broadcasted_iota(jnp.int32, (16, 128), 1)


def lower(rows=16):
    return lax.broadcasted_iota(jnp.int32, (rows, 128), 1) < 64


def half_turn(v):
    return pltpu.roll(v, 64, 1)


def inside(j, k, sign):
    lane = lanes()
    y = (lane // 8) % 8 + sign * (j - 1)
    z = lane % 8 + sign * (k - 1)
    return (y >= 0) & (y < 8) & (z >= 0) & (z < 8)


def shifted(v, j, k, sign):
    delta = sign * (8 * (j - 1) + (k - 1))
    if delta == 0:
        return v
    parts = v.shape[0] // 16
    keep = inside(j, k, sign)
    if parts > 1:
        keep = jnp.concatenate([keep] * parts, axis=0)
    return jnp.where(keep, pltpu.roll(v, (-delta) % 128, 1), 0.0)


def regroup(w_ref, z_ref):
    group = lanes() // 16
    for q in range(4):
        for h in range(2):
            tiles = []
            for i in range(8):
                tap = 8 * q + i
                if tap < TAPS:
                    tiles.append(w_ref[16 * tap : 16 * tap + 16, 128 * h : 128 * h + 128].astype(F32))
                else:
                    tiles.append(jnp.zeros((16, 128), F32))
            for bit in (1, 2, 4):
                low = (group & bit) == 0
                for i in range(8):
                    if i & bit:
                        continue
                    a, b = tiles[i], tiles[i + bit]
                    tiles[i] = jnp.where(low, a, pltpu.roll(b, 16 * bit, 1))
                    tiles[i + bit] = jnp.where(low, pltpu.roll(a, 128 - 16 * bit, 1), b)
            for i in range(8):
                z_ref[8 * h + i, :, 128 * q : 128 * q + 128] = tiles[i].astype(BF16)


def gather_taps(y_ref, p_ref, hm_ref, hp_ref, sign):
    lo = lower()
    lefts = []
    for half in range(2):
        at = slice(128 * half, 128 * half + 128)
        total = None
        for j in range(3):
            for k in range(3):
                rows = [16 * (9 * i + 3 * j + k) for i in range(3)]
                first, mid, last = [y_ref[r : r + 16, at] for r in rows]
                if sign < 0:
                    first, last = last, first
                inner = jnp.where(lo, first, last)
                outer = jnp.where(lo, last, first)
                term = shifted(jnp.concatenate([mid, inner, outer], axis=0), j, k, sign)
                total = term if total is None else total + term
        p_ref[:, at] = total[:16] + half_turn(total[16:32])
        lefts.append(total[32:])
    hm_ref[...] = jnp.where(lo, lefts[0], half_turn(lefts[1]))
    hp_ref[...] = jnp.where(lo, half_turn(lefts[0]), lefts[1])


def spread_halo(hp, hm, first, final):
    lo = lower(hp.shape[0])
    hp = jnp.where(first, 0.0, hp.astype(F32))
    hm = jnp.where(final, 0.0, hm.astype(F32))
    return [jnp.where(lo, hp, half_turn(hm)), jnp.where(lo, half_turn(hp), hm)]


def edge_planes(v):
    lo = lower(v.shape[0])
    a, b = v[:, :128], v[:, 128:]
    return jnp.where(lo, a, half_turn(b)), jnp.where(lo, half_turn(a), b)


def scatter_taps(v, halos, im_ref):
    lo = lower()
    for half in range(2):
        at = slice(128 * half, 128 * half + 128)
        own = v[:, at]
        turned = half_turn(own)
        stack = jnp.concatenate(
            [jnp.where(lo, halos[half], turned), own, jnp.where(lo, turned, halos[half])], axis=0
        )
        for j in range(3):
            for k in range(3):
                term = shifted(stack, j, k, 1).astype(BF16)
                for i in range(3):
                    row = 16 * (9 * i + 3 * j + k)
                    im_ref[row : row + 16, at] = term[16 * i : 16 * i + 16]


def kernel(
    factor,
    x_hbm, g_hbm, w1_hbm, w2_hbm,
    out_ref, gin_ref, one_ref, two_ref,
    x_ref, g_ref, w1, w2,
    ga, gb, z1, z2, r1, r2, f1, f2, y_ref, p_ref, hm, hp, rhm, rhp,
    xm, xp, rxm, rxp, am, ap, ram, rap, imx, ima, gsum, gout, gin2, mine, sent, rr, part, other, full, oc, oall,
    in_sem, w_send, w_recv, v_send, v_recv, a_send, a_recv,
    h_send, h_recv, n_send, n_recv, c_send, c_recv, r_send, r_recv, x_send, x_recv, f_send, f_recv, o_send, o_recv,
):
    d = lax.axis_index("dp")
    s = lax.axis_index("space")
    m, e = d // 2, d % 2
    xl, y = m // 4, m % 4
    z, xh = s // 2, s % 2
    above = lax.rem(s + 1, 16)
    below = lax.rem(s + 15, 16)
    first, final = s == 0, s == 15
    sibling = 2 * m + 1 - e
    up, down, far = [lax.rem(y + step, 4) for step in (1, 3, 2)]
    side = (1 - xl) * 4
    U, D, O, X = xl * 4 + up, xl * 4 + down, xl * 4 + far, side + y
    XU, XD, XO = side + up, side + down, side + far
    channels = pl.ds(pl.multiple_of(m * 32, 32), 32)

    def rows_of(index, count):
        return pl.ds(pl.multiple_of(index * count, count), count)

    def remote(src, dst, send, recv, dp, space):
        return pltpu.make_async_remote_copy(
            src_ref=src, dst_ref=dst, send_sem=send, recv_sem=recv, device_id=(dp, space), device_id_type=MESH
        )

    def each(count, body, start=0):
        def step(i, carry):
            body(i)
            return carry

        lax.fori_loop(start, count, step, 0)

    barrier = pltpu.get_barrier_semaphore()

    def greet(dp, space):
        pl.semaphore_signal(barrier, inc=1, device_id=(dp, space), device_id_type=MESH)

    each(8, lambda r: greet(2 * lax.rem(m + r, 8) + e, s), 1)
    each(8, lambda r: greet(d, 2 * lax.rem(z + r, 8) + xh), 1)
    greet(sibling, s)
    greet(d, above)
    greet(d, below)

    pairs = [(x_hbm, x_ref), (g_hbm, g_ref), (w1_hbm, w1.at[e]), (w2_hbm, w2.at[e])]
    loads = [pltpu.make_async_copy(src, dst, in_sem.at[i]) for i, (src, dst) in enumerate(pairs)]
    for load in loads:
        load.start()

    def block(phase, t, chip):
        if phase == 0:
            return ga.at[chip // 2, t, :, pl.ds(pl.multiple_of(lax.rem(chip, 2) * 128, 128), 128)]
        return gb.at[t, :, rows_of(chip, 32), :]

    HOPS = [(m, X, X), (m, U, D), (m, D, U), (m, O, O), (X, U, XD), (X, D, XU), (O, X, XO)]

    def hop(phase, t, kind):
        chip, to, _ = HOPS[kind]
        ref = block(phase, t, chip)
        return remote(ref, ref, a_send.at[phase, t, kind], a_recv.at[phase, t, kind], 2 * to + e, s)

    def landed(phase, t, *kinds):
        for kind in kinds:
            _, to, chip = HOPS[kind]
            ref = block(phase, t, chip)
            remote(ref, ref, a_send.at[phase, t, kind], a_recv.at[phase, t, kind], 2 * to + e, s).wait_recv()

    def depart(phase, t):
        for kind in range(4):
            hop(phase, t, kind).start()

    def relay(phase, t):
        landed(phase, t, 0)
        hop(phase, t, 4).start()
        hop(phase, t, 5).start()
        landed(phase, t, 3)
        hop(phase, t, 6).start()

    def slices(which, src, r, to, source):
        return remote(
            src.at[pl.ds(2 * to, 2)], r.at[:, source, e], w_send.at[which, to], w_recv.at[which, source], 2 * to + e, s
        )

    def cores(index, src, dst):
        return remote(src, dst, v_send.at[index], v_recv.at[index], sibling, s)

    def send_slices(which, src, r):
        each(8, lambda step: slices(which, src, r, lax.rem(m + step, 8), m).start(), 1)
        for slot in range(2):
            r[slot, m, e] = src[2 * m + slot]

    def pass_slices(which, src, r):
        def body(step):
            at = lax.rem(m + 8 - step, 8)
            slices(which, src, r, at, at).wait_recv()

        each(8, body, 1)
        cores(which, r.at[:, :, e], r.at[:, :, e]).start()

    def wait_slices(which, r, f):
        cores(which, r.at[:, :, 1 - e], r.at[:, :, 1 - e]).wait_recv()
        for slot in range(2):
            f[slot] = r[slot].reshape(C, 512).astype(F32).T.astype(BF16)

    mine_at = pl.ds(pl.multiple_of(lax.rem(m, 2) * 128, 128), 128)
    loads[0].wait()
    ga[m // 2, 0, :, mine_at] = x_ref[...].astype(F32).T.astype(BF16)
    loads[1].wait()
    ga[m // 2, 1, :, mine_at] = g_ref[...].astype(F32).T.astype(BF16)
    loads[2].wait()
    regroup(w1.at[e], z1)
    loads[3].wait()
    regroup(w2.at[e], z2)
    sent[:, TILES:] = jnp.zeros((2, 8 * SHARE - TILES, 16, 128), BF16)
    mine[:, TILES:] = jnp.zeros((2, 8 * SHARE - TILES, 16, 128), F32)
    pl.semaphore_wait(barrier, 17)

    depart(0, 0)
    send_slices(0, z1, r1)
    depart(0, 1)
    cores(2, w2.at[e], w2.at[e]).start()
    cores(3, w1.at[e], w1.at[e]).start()
    landed(0, 0, 0)
    hop(0, 0, 4).start()
    hop(0, 0, 5).start()
    pass_slices(0, z1, r1)
    landed(0, 0, 3)
    hop(0, 0, 6).start()
    relay(0, 1)
    wait_slices(0, r1, f1)
    cores(2, w2.at[1 - e], w2.at[1 - e]).wait_recv()

    def halo_copies(phase, pair):
        return (
            remote(hm.at[phase, pair], rhm.at[phase, pair], h_send.at[phase, 0, pair], h_recv.at[phase, 0, pair], d, below),
            remote(hp.at[phase, pair], rhp.at[phase, pair], h_send.at[phase, 1, pair], h_recv.at[phase, 1, pair], d, above),
        )

    own_pair, other_pair = xl * 2 + y // 2, xl * 2 + 1 - y // 2
    ORDER = [own_pair, other_pair, side // 2 + y // 2, side // 2 + 1 - y // 2]

    def pair_at(i):
        pair = ORDER[0]
        for at in range(1, 4):
            pair = jnp.where(i == at, ORDER[at], pair)
        return pair

    def convolve(phase, pair, f, v, w, g):
        for slot in range(2):
            rows = pl.ds(16 * slot, 16)
            for t in range(2):
                y = y_ref.at[2 * slot + t]
                y[...] = dot(f[slot, :ROWS], v()) if t == 0 else dot(w[slot], g())
                gather_taps(
                    y, p_ref.at[t, pair, rows], hm.at[phase, pair, t, rows], hp.at[phase, pair, t, rows], 1 - 2 * t
                )
        for copy in halo_copies(phase, pair):
            copy.start()

    def phase_one(i):
        for at, kinds in enumerate(((1, 2), (3,), (0, 4, 5), (6,))):
            @pl.when(i == at)
            def _():
                for t in range(2):
                    landed(0, t, *[kind for kind in kinds if kind not in (0, 3)])

        pair = pair_at(i)
        convolve(0, pair, f1, lambda: ga[pair, 0], w2, lambda: ga[pair, 1])

    each(4, phase_one)
    send_slices(1, z2, r2)

    def near(index, src, dst, to):
        return remote(src, dst, n_send.at[index], n_recv.at[index], d, to)

    def x_edges(pair):
        lowest, highest = edge_planes(ga[pair, 0, channels, :].astype(F32))
        xm[pair] = lowest.astype(BF16)
        xp[pair] = highest.astype(BF16)

    each(4, x_edges)

    def halo_of(phase, t, pair):
        return jnp.concatenate(spread_halo(rhp[phase, pair, t], rhm[phase, pair, t], first, final), axis=1)

    def middle(i):
        pair = pair_at(i)
        for copy in halo_copies(0, pair):
            copy.wait_recv()
        pre = p_ref[0, pair] + halo_of(0, 0, pair)
        grad = p_ref[1, pair] + halo_of(0, 1, pair)
        sig = jax.nn.sigmoid(pre)
        act = (pre * sig).astype(BF16)
        gb[0, pair, channels, :] = act
        gb[1, pair, channels, :] = (grad * sig * (1.0 + pre * (1.0 - sig))).astype(BF16)
        lowest, highest = edge_planes(act.astype(F32))
        am[pair] = lowest.astype(BF16)
        ap[pair] = highest.astype(BF16)

    each(4, middle)
    depart(1, 1)
    near(2, am, ram, below).start()
    near(3, ap, rap, above).start()
    depart(1, 0)
    near(0, xm, rxm, below).start()
    near(1, xp, rxp, above).start()

    def taps(pair, v, up_halo, down_halo, im):
        for slot in range(2):
            rows = slice(16 * slot, 16 * slot + 16)
            halos = spread_halo(up_halo[pair, rows], down_halo[pair, rows], first, final)
            scatter_taps(v[rows], halos, im.at[pair, slot])

    def taps_x(pair):
        taps(pair, ga[pair, 0, channels, :].astype(F32), rxp, rxm, imx)

    def taps_a(pair):
        taps(pair, gb[0, pair, channels, :].astype(F32), rap, ram, ima)

    def core_copy(which):
        return remote(gout.at[which], gin2.at[which], c_send.at[which], c_recv.at[which], sibling, s)

    def reduce_copy(which, step):
        to = lax.rem(z + step, 8)
        return remote(
            sent.at[which, pl.ds(to * SHARE, SHARE)], rr.at[which, step],
            r_send.at[which, step], r_recv.at[which, step], d, 2 * to + xh,
        )

    def product(im, slot, operand, total):
        total[...] = dot(im[0, slot], operand(0), ((1,), (1,)))

        def add(pair):
            total[...] += dot(im[pair, slot], operand(pair), ((1,), (1,)))

        each(4, add, 1)

    def send_partial(which, im, operand):
        product(im, 1 - e, operand, gout.at[which])
        core_copy(which).start()
        product(im, e, operand, gsum)
        core_copy(which).wait_recv()
        for tile in range(TILES):
            row, lane = tile // 2 * 16, tile % 2 * 128
            at = (slice(row, row + 16), slice(lane, lane + 128))
            value = gsum[at] + gin2[(which, *at)]
            mine[which, tile] = value
            sent[which, tile] = value.astype(BF16)
        each(8, lambda step: reduce_copy(which, step).start(), 1)

    def pair_copy(which):
        return remote(part.at[which], other.at[which], x_send.at[which], x_recv.at[which], d, 2 * z + 1 - xh)

    def reduce_ring(which):
        each(8, lambda step: reduce_copy(which, step).wait_recv(), 1)
        total = mine[which, pl.ds(z * SHARE, SHARE)]
        for step in range(1, 8):
            total += rr[which, step].astype(F32)
        part[which] = total
        pair_copy(which).start()

    CUT = SHARE // 2 + 1
    STEPS = [
        (0, 0, SHARE, 2), (0, 0, SHARE, -2),
        (-2, 0, SHARE, -1), (-2, 0, SHARE, 1), (2, 0, SHARE, 1), (2, 0, SHARE, -1),
        (-2, 0, CUT, 2), (2, CUT, SHARE, -2),
    ]

    def spread_copy(which, kind, arriving=False):
        owner, low, high, far_to = STEPS[kind]
        if arriving:
            owner = owner - far_to
        ref = full.at[which, pl.ds(lax.rem(z + owner + 8, 8) * SHARE + low, high - low)]
        to = 2 * lax.rem(z + far_to + 8, 8) + xh
        return remote(ref, ref, f_send.at[which, kind], f_recv.at[which, kind], d, to)

    def spread(which):
        pair_copy(which).wait_recv()
        full[which, pl.ds(z * SHARE, SHARE)] = (part[which] + other[which]) * factor
        spread_copy(which, 0).start()
        spread_copy(which, 1).start()

    def spread_on(which):
        for kind, then in ((0, (3, 2, 6)), (1, (5, 4, 7))):
            spread_copy(which, kind, True).wait_recv()
            for more in then:
                spread_copy(which, more).start()

    def gradient_out(which, ref):
        for kind in range(2, 8):
            spread_copy(which, kind, True).wait_recv()
        for tile in range(TILES):
            row, lane = tile // 2 * 16, tile % 2 * 128
            ref[row : row + 16, lane : lane + 128] = full[which, tile]

    relay(1, 1)
    near(2, am, ram, below).wait_recv()
    near(3, ap, rap, above).wait_recv()
    each(4, taps_a)
    relay(1, 0)
    send_partial(1, ima, lambda pair: ga[pair, 1])
    near(0, xm, rxm, below).wait_recv()
    near(1, xp, rxp, above).wait_recv()
    each(4, taps_x)
    landed(1, 1, 1, 2, 4, 5, 6)
    send_partial(0, imx, lambda pair: gb[1, pair])
    pass_slices(1, z2, r2)
    reduce_ring(1)
    landed(1, 0, 1, 2, 4, 5, 6)
    wait_slices(1, r2, f2)
    cores(3, w1.at[1 - e], w1.at[1 - e]).wait_recv()

    def phase_two(i):
        @pl.when(i == 2)
        def _():
            spread(1)

        pair = pair_at(i)
        convolve(1, pair, f2, lambda: gb[0, pair], w1, lambda: gb[1, pair])

    each(4, phase_two)
    reduce_ring(0)
    spread_on(1)

    def home(to, source):
        return remote(oc.at[to], oall.at[source], o_send.at[to], o_recv.at[source], 2 * to + e, s)

    def finish(i):
        pair = pair_at(i)
        for copy in halo_copies(1, pair):
            copy.wait_recv()
        for t in range(2):
            total = p_ref[t, pair] + halo_of(1, t, pair)
            total = (ga[pair, t, channels, :].astype(F32) + total).astype(BF16)
            oc[2 * pair, t] = total[:, :128]
            oc[2 * pair + 1, t] = total[:, 128:]
        for half in range(2):
            to = 2 * pair + half

            @pl.when(to != m)
            def _():
                home(to, m).start()

    each(4, finish)
    spread(0)
    oall[m] = oc[m]

    def wait_home(step):
        source = lax.rem(m + 8 - step, 8)
        home(source, source).wait_recv()

    each(8, wait_home, 1)
    out_ref[...] = oall[:, 0].reshape(C, 128).astype(F32).T.astype(BF16)
    gin_ref[...] = oall[:, 1].reshape(C, 128).astype(F32).T.astype(BF16)
    spread_on(0)
    gradient_out(1, two_ref)
    gradient_out(0, one_ref)

    def wait_far(step):
        to = lax.rem(m + step, 8)
        home(to, m).wait_send()
        slices(0, z1, r1, to, m).wait_send()
        slices(1, z2, r2, to, m).wait_send()
        for which in range(2):
            reduce_copy(which, step).wait_send()

    each(8, wait_far, 1)

    def wait_halo(pair):
        for phase in range(2):
            for copy in halo_copies(phase, pair):
                copy.wait_send()

    each(4, wait_halo)
    cores(0, r1.at[:, :, e], r1.at[:, :, e]).wait_send()
    cores(1, r2.at[:, :, e], r2.at[:, :, e]).wait_send()
    cores(2, w2.at[e], w2.at[e]).wait_send()
    cores(3, w1.at[e], w1.at[e]).wait_send()
    for t in range(2):
        core_copy(t).wait_send()
        pair_copy(t).wait_send()
        for kind in range(8):
            spread_copy(t, kind).wait_send()
        for phase in range(2):
            for kind in range(7):
                hop(phase, t, kind).wait_send()
    near(0, xm, rxm, below).wait_send()
    near(1, xp, rxp, above).wait_send()
    near(2, am, ram, below).wait_send()
    near(3, ap, rap, above).wait_send()


def shards(features, weight_one, weight_two, cotangent):
    shape = features.shape
    count = shape[0] * lax.axis_size("dp") * shape[1] * lax.axis_size("space") * shape[2] * shape[3]
    factor = float(count) ** (-0.5)
    vmem = pl.BlockSpec(memory_space=pltpu.VMEM)
    dma = pltpu.SemaphoreType.DMA
    scratch = pltpu.VMEM
    out, gin, one, two = pl.pallas_call(
        functools.partial(kernel, factor),
        out_shape=[
            jax.ShapeDtypeStruct((128, C), BF16),
            jax.ShapeDtypeStruct((128, C), BF16),
            jax.ShapeDtypeStruct((ROWS, C), F32),
            jax.ShapeDtypeStruct((ROWS, C), F32),
        ],
        in_specs=[pl.BlockSpec(memory_space=pl.ANY)] * 4,
        out_specs=[vmem] * 4,
        scratch_shapes=[
            scratch((128, C), BF16), scratch((128, C), BF16),
            scratch((2, ROWS, C), BF16), scratch((2, ROWS, C), BF16),
            scratch((4, 2, C, C), BF16),
            scratch((2, 4, C, C), BF16),
            scratch((16, 16, 512), BF16), scratch((16, 16, 512), BF16),
            scratch((2, 8, 2, 16, 512), BF16), scratch((2, 8, 2, 16, 512), BF16),
            scratch((2, 512, C), BF16), scratch((2, 512, C), BF16),
            scratch((4, ROWS, C), F32),
            scratch((2, 4, 32, C), F32),
            *[scratch((2, 4, 2, 32, 128), F32)] * 4,
            *[scratch((4, 32, 128), BF16)] * 8,
            scratch((4, 2, ROWS, C), BF16), scratch((4, 2, ROWS, C), BF16),
            scratch((ROWS, C), F32),
            scratch((2, ROWS, C), F32), scratch((2, ROWS, C), F32),
            scratch((2, 8 * SHARE, 16, 128), F32),
            scratch((2, 8 * SHARE, 16, 128), BF16),
            scratch((2, 8, SHARE, 16, 128), BF16),
            scratch((2, SHARE, 16, 128), F32), scratch((2, SHARE, 16, 128), F32),
            scratch((2, 8 * SHARE, 16, 128), F32),
            scratch((8, 2, 32, 128), BF16), scratch((8, 2, 32, 128), BF16),
            dma((4,)),
            dma((2, 8)), dma((2, 8)), dma((4,)), dma((4,)),
            dma((2, 2, 7)), dma((2, 2, 7)),
            dma((2, 2, 4)), dma((2, 2, 4)),
            dma((4,)), dma((4,)), dma((2,)), dma((2,)),
            dma((2, 8)), dma((2, 8)), dma((2,)), dma((2,)), dma((2, 8)), dma((2, 8)),
            dma((8,)), dma((8,)),
        ],
        compiler_params=pltpu.CompilerParams(
            collective_id=0, has_side_effects=True, vmem_limit_bytes=56 * 2**20
        ),
    )(
        features.reshape(128, C), cotangent.reshape(128, C),
        weight_one.reshape(ROWS, C), weight_two.reshape(ROWS, C),
    )
    return out.reshape(shape), gin.reshape(shape), one.reshape(TAPS, 16, C), two.reshape(TAPS, 16, C)


def solution(mesh):
    in_specs = (
        P("dp", "space", None, None, None),
        P(None, "dp", None),
        P(None, "dp", None),
        P("dp", "space", None, None, None),
    )
    out_specs = (
        P("dp", "space", None, None, None),
        P("dp", "space", None, None, None),
        P(None, "dp", None),
        P(None, "dp", None),
    )
    return jax.shard_map(shards, mesh=mesh, in_specs=in_specs, out_specs=out_specs, check_vma=False)
```

time: 428 us -> 82.8 us (0.19)
  waiting for transfers between devices: 321 us -> 0 us
  Pallas kernels: 0 us -> 77.2 us
  local copies, waits for them, and re-layouts: 38.1 us -> 4.76 us
  starting transfers between devices: 30.8 us -> 0 us
  between operations: 14.8 us -> 0.65 us
  other arithmetic: 12.9 us -> 0 us
  matrix products: 8.85 us -> 0 us
    psum x1 -> x0, waiting for transfers between devices: 161 us -> none  [kernel_grad(): return lax.psum(share, 'space') * factor]
    reduce_scatter x2 -> x0, waiting for transfers between devices: 105 us -> none  [kernel_grad(): lax.psum_scatter(weight_terms(pad_across(frame), grad_out), 'dp', scatter...]
    pallas_call x0 -> x1, Pallas kernels: none -> 77.2 us  [shards(): pl.pallas_call(functools.partial(kernel, factor), out_shape=[jax.ShapeDty...]
    all_gather x2 -> x0, waiting for transfers between devices: 52.8 us -> none  [forward_rows(): gathered = lax.all_gather(shard, 'dp', axis=1, tiled=True)]
    ppermute x8 -> x0, starting transfers between devices: 30.6 us -> none  [the longest x4 25.5 us: padded_2(): lax.ppermute(tail, axis, [(i, (i + 1) % count) for i in range(ends)])]
    slice x14 -> x0, local copies, waits for them, and re-layouts: 22.7 us -> none  [the longest x10 19.5 us: convolve(): block = kernel[9 * plane:9 * plane + 9].reshape(9 * chans, -1)]
    dot_general x18 -> x0, matrix products: 8.85 us -> none  [the longest x12 5.89 us: convolve(): jnp.dot(stencil_taps(padded, plane), block, preferred_element_type=jnp.fl...]
    concatenate x6 -> x0, other arithmetic: 8.49 us -> none  [the longest x2 6.42 us: weight_terms(): return jnp.concatenate(parts, axis=0).reshape(27, chans, flat.shape[1])]
  transfers between devices with their start and end apart: 13 -> 0, of which waited for: 6 -> 0; matrix products, arithmetic and copies ran while one was open for 10% -> 0% of each run, Pallas kernels for 0% -> 0%
where the time goes in v2:
time: 82.8 us; the launch traced here: 82.6 us
  Pallas kernels  77.2 us (93%)
  local copies, waits for them, and re-layouts  4.76 us (6%)
    pallas_call x1, Pallas kernels, shards(): pl.pallas_call(functools.partial(kernel, factor), out_shape=[jax.ShapeDty...  77.2 us
    unnamed x8, local copies, waits for them, and re-layouts  4.76 us

profile of v2, /device:TPU:24, one launch (start us, length us, event | category | flops | bytes accessed | tf_op | source)
XLA Modules:
  0.0 82.6 jit_solution(3673864647735376791)
XLA Ops:
  0.6 77.2 %shard_map.75 = (bf16[128,256]{1,0:T(8,128)(2,1)}, bf16[128,256]{1,0:T(8,128)(2,1)}, f32[432,256]{1,0:T(8,128)}, f32[432,256]{1,0:T(8,128)}) custom-call(bf16[128,256]{1,0:T(8,128)(2,1)} %bitcast.12, bf16[128,256]{1,0:T(8,128)(2,1)} %bitcast.13, bf16[432,256]{1,0:T(8,128)(2,1)} %bitcast.10, bf16[432,256]{1,0:T(8,128)(2,1)} %bitcast.11), custom_call_target="tpu_custom_call" | custom-call | tf_op jit(solution)/shard_map/pallas_call | solution.py:535
  77.8 0.0 copy-start.1
  77.8 1.5 %copy.12 = bf16[1,2,8,8,256]{4,3,2,1,0:T(8,128)(2,1)} copy(bf16[1,2,8,8,256]{4,3,2,1,0:T(8,128)(2,1)} %bitcast.15) | data formatting | bytes 131072
  79.3 0.0 copy-done.1
  79.3 0.6 copy.13
  80.0 0.0 copy-start
  80.0 1.9 %copy.14 = f32[27,16,256]{2,1,0:T(8,128)} copy(f32[27,16,256]{2,1,0:T(8,128)} %bitcast.9) | data formatting | bytes 884736
  81.8 0.0 copy-done
  81.8 0.8 copy.15
Async XLA Ops:
  77.8 1.5 %copy-start.1 = (bf16[128,256]{1,0:T(8,128)(2,1)S(1)}, bf16[128,256]{1,0:T(8,128)(2,1)}, u32[]{:S(2)}) copy-start(bf16[128,256]{1,0:T(8,128)(2,1)} %get-tuple-element.9) | copy-start | bytes 196612
  80.0 1.9 %copy-start = (f32[432,256]{1,0:T(8,128)S(1)}, f32[432,256]{1,0:T(8,128)}, u32[]{:S(2)}) copy-start(f32[432,256]{1,0:T(8,128)} %get-tuple-element.11) | copy-start | bytes 1327108

commit v3 on v2

--- a/solution.py
+++ b/solution.py
@@ -129,11 +129,11 @@
 def kernel(
     factor,
     x_hbm, g_hbm, w1_hbm, w2_hbm,
-    out_ref, gin_ref, one_ref, two_ref,
+    cells_hbm, grads_hbm,
     x_ref, g_ref, w1, w2,
     ga, gb, z1, z2, r1, r2, f1, f2, y_ref, p_ref, hm, hp, rhm, rhp,
     xm, xp, rxm, rxp, am, ap, ram, rap, imx, ima, gsum, gout, gin2, mine, sent, rr, part, other, full, oc, oall,
-    in_sem, w_send, w_recv, v_send, v_recv, a_send, a_recv,
+    in_sem, out_sem, w_send, w_recv, v_send, v_recv, a_send, a_recv,
     h_send, h_recv, n_send, n_recv, c_send, c_recv, r_send, r_recv, x_send, x_recv, f_send, f_recv, o_send, o_recv,
 ):
     d = lax.axis_index("dp")
@@ -145,6 +145,7 @@
     below = lax.rem(s + 15, 16)
     first, final = s == 0, s == 15
     sibling = 2 * m + 1 - e
+    across = 2 * z + 1 - xh
     up, down, far = [lax.rem(y + step, 4) for step in (1, 3, 2)]
     side = (1 - xl) * 4
     U, D, O, X = xl * 4 + up, xl * 4 + down, xl * 4 + far, side + y
@@ -176,6 +177,7 @@
     greet(sibling, s)
     greet(d, above)
     greet(d, below)
+    each(4, lambda r: greet(2 * (side + r) + e, across))
 
     pairs = [(x_hbm, x_ref), (g_hbm, g_ref), (w1_hbm, w1.at[e]), (w2_hbm, w2.at[e])]
     loads = [pltpu.make_async_copy(src, dst, in_sem.at[i]) for i, (src, dst) in enumerate(pairs)]
@@ -187,33 +189,42 @@
             return ga.at[chip // 2, t, :, pl.ds(pl.multiple_of(lax.rem(chip, 2) * 128, 128), 128)]
         return gb.at[t, :, rows_of(chip, 32), :]
 
-    HOPS = [(m, X, X), (m, U, D), (m, D, U), (m, O, O), (X, U, XD), (X, D, XU), (O, X, XO)]
-
-    def hop(phase, t, kind):
-        chip, to, _ = HOPS[kind]
-        ref = block(phase, t, chip)
+    HOPS = [
+        (m, None, X, X), (m, None, U, D), (m, None, D, U), (X, None, U, XD), (X, None, D, XU),
+        (D, 0, U, O), (U, 1, D, O), (XD, 0, U, XO), (XU, 1, D, XO),
+    ]
+
+    def hop(phase, t, kind, arriving=False):
+        chip, half, to, source = HOPS[kind]
+        ref = block(phase, t, source if arriving else chip)
+        if half is not None:
+            ref = ref.at[pl.ds(128 * half, 128)] if phase == 0 else ref.at[pl.ds(2 * half, 2)]
         return remote(ref, ref, a_send.at[phase, t, kind], a_recv.at[phase, t, kind], 2 * to + e, s)
 
     def landed(phase, t, *kinds):
         for kind in kinds:
-            _, to, chip = HOPS[kind]
-            ref = block(phase, t, chip)
-            remote(ref, ref, a_send.at[phase, t, kind], a_recv.at[phase, t, kind], 2 * to + e, s).wait_recv()
+            hop(phase, t, kind, True).wait_recv()
 
     def depart(phase, t):
-        for kind in range(4):
+        for kind in range(3):
             hop(phase, t, kind).start()
 
     def relay(phase, t):
-        landed(phase, t, 0)
-        hop(phase, t, 4).start()
-        hop(phase, t, 5).start()
-        landed(phase, t, 3)
-        hop(phase, t, 6).start()
+        for kind, then in ((0, (3, 4)), (1, (5,)), (2, (6,))):
+            landed(phase, t, kind)
+            for more in then:
+                hop(phase, t, more).start()
+
+    def relay_more(phase, t):
+        for kind, more in ((3, 7), (4, 8)):
+            landed(phase, t, kind)
+            hop(phase, t, more).start()
 
     def slices(which, src, r, to, source):
+        space = jnp.where(to // 4 == xl, s, across)
         return remote(
-            src.at[pl.ds(2 * to, 2)], r.at[:, source, e], w_send.at[which, to], w_recv.at[which, source], 2 * to + e, s
+            src.at[pl.ds(2 * to, 2)], r.at[:, source, e],
+            w_send.at[which, to], w_recv.at[which, source], 2 * to + e, space,
         )
 
     def cores(index, src, dst):
@@ -248,20 +259,16 @@
     regroup(w2.at[e], z2)
     sent[:, TILES:] = jnp.zeros((2, 8 * SHARE - TILES, 16, 128), BF16)
     mine[:, TILES:] = jnp.zeros((2, 8 * SHARE - TILES, 16, 128), F32)
-    pl.semaphore_wait(barrier, 17)
+    pl.semaphore_wait(barrier, 21)
 
     depart(0, 0)
     send_slices(0, z1, r1)
     depart(0, 1)
     cores(2, w2.at[e], w2.at[e]).start()
-    cores(3, w1.at[e], w1.at[e]).start()
-    landed(0, 0, 0)
-    hop(0, 0, 4).start()
-    hop(0, 0, 5).start()
+    relay(0, 0)
     pass_slices(0, z1, r1)
-    landed(0, 0, 3)
-    hop(0, 0, 6).start()
     relay(0, 1)
+    relay_more(0, 0)
     wait_slices(0, r1, f1)
     cores(2, w2.at[1 - e], w2.at[1 - e]).wait_recv()
 
@@ -293,16 +300,19 @@
             copy.start()
 
     def phase_one(i):
-        for at, kinds in enumerate(((1, 2), (3,), (0, 4, 5), (6,))):
+        for at, kinds in ((1, (5, 6)), (3, (7, 8))):
             @pl.when(i == at)
             def _():
+                if at == 1:
+                    relay_more(0, 1)
                 for t in range(2):
-                    landed(0, t, *[kind for kind in kinds if kind not in (0, 3)])
+                    landed(0, t, *kinds)
 
         pair = pair_at(i)
         convolve(0, pair, f1, lambda: ga[pair, 0], w2, lambda: ga[pair, 1])
 
     each(4, phase_one)
+    cores(3, w1.at[e], w1.at[e]).start()
     send_slices(1, z2, r2)
 
     def near(index, src, dst, to):
@@ -411,7 +421,7 @@
 
     def spread(which):
         pair_copy(which).wait_recv()
-        full[which, pl.ds(z * SHARE, SHARE)] = (part[which] + other[which]) * factor
+        full[which, pl.ds(z * SHARE, SHARE)] = ((part[which] + other[which]) * factor).astype(BF16)
         spread_copy(which, 0).start()
         spread_copy(which, 1).start()
 
@@ -421,41 +431,44 @@
             for more in then:
                 spread_copy(which, more).start()
 
-    def gradient_out(which, ref):
+    def result(which):
+        src, dst = (oall, cells_hbm) if which == 2 else (full.at[which], grads_hbm.at[which])
+        return pltpu.make_async_copy(src, dst, out_sem.at[which])
+
+    def spread_end(which):
         for kind in range(2, 8):
             spread_copy(which, kind, True).wait_recv()
-        for tile in range(TILES):
-            row, lane = tile // 2 * 16, tile % 2 * 128
-            ref[row : row + 16, lane : lane + 128] = full[which, tile]
+        result(which).start()
 
     relay(1, 1)
     near(2, am, ram, below).wait_recv()
     near(3, ap, rap, above).wait_recv()
     each(4, taps_a)
     relay(1, 0)
+    relay_more(1, 1)
     send_partial(1, ima, lambda pair: ga[pair, 1])
     near(0, xm, rxm, below).wait_recv()
     near(1, xp, rxp, above).wait_recv()
     each(4, taps_x)
-    landed(1, 1, 1, 2, 4, 5, 6)
+    relay_more(1, 0)
+    landed(1, 1, 5, 6, 7, 8)
     send_partial(0, imx, lambda pair: gb[1, pair])
     pass_slices(1, z2, r2)
-    reduce_ring(1)
-    landed(1, 0, 1, 2, 4, 5, 6)
+    landed(1, 0, 5, 6, 7, 8)
     wait_slices(1, r2, f2)
     cores(3, w1.at[1 - e], w1.at[1 - e]).wait_recv()
 
     def phase_two(i):
         @pl.when(i == 2)
         def _():
-            spread(1)
+            reduce_ring(1)
 
         pair = pair_at(i)
         convolve(1, pair, f2, lambda: gb[0, pair], w1, lambda: gb[1, pair])
 
     each(4, phase_two)
+    spread(1)
     reduce_ring(0)
-    spread_on(1)
 
     def home(to, source):
         return remote(oc.at[to], oall.at[source], o_send.at[to], o_recv.at[source], 2 * to + e, s)
@@ -478,6 +491,7 @@
 
     each(4, finish)
     spread(0)
+    spread_on(1)
     oall[m] = oc[m]
 
     def wait_home(step):
@@ -485,11 +499,12 @@
         home(source, source).wait_recv()
 
     each(8, wait_home, 1)
-    out_ref[...] = oall[:, 0].reshape(C, 128).astype(F32).T.astype(BF16)
-    gin_ref[...] = oall[:, 1].reshape(C, 128).astype(F32).T.astype(BF16)
+    result(2).start()
     spread_on(0)
-    gradient_out(1, two_ref)
-    gradient_out(0, one_ref)
+    spread_end(1)
+    spread_end(0)
+    for which in range(3):
+        result(which).wait()
 
     def wait_far(step):
         to = lax.rem(m + step, 8)
@@ -517,12 +532,21 @@
         for kind in range(8):
             spread_copy(t, kind).wait_send()
         for phase in range(2):
-            for kind in range(7):
+            for kind in range(9):
                 hop(phase, t, kind).wait_send()
     near(0, xm, rxm, below).wait_send()
     near(1, xp, rxp, above).wait_send()
     near(2, am, ram, below).wait_send()
     near(3, ap, rap, above).wait_send()
+
+
+def lay_out(cells_ref, grads_ref, out_ref, gin_ref, one_ref, two_ref):
+    for t, ref in enumerate((out_ref, gin_ref)):
+        ref[...] = cells_ref[:, t].reshape(C, 128).astype(F32).T.astype(BF16)
+    for which, ref in enumerate((one_ref, two_ref)):
+        for tile in range(TILES):
+            row, lane = tile // 2 * 16, tile % 2 * 128
+            ref[row : row + 16, lane : lane + 128] = grads_ref[which, tile].astype(F32)
 
 
 def shards(features, weight_one, weight_two, cotangent):
@@ -532,16 +556,14 @@
     vmem = pl.BlockSpec(memory_space=pltpu.VMEM)
     dma = pltpu.SemaphoreType.DMA
     scratch = pltpu.VMEM
-    out, gin, one, two = pl.pallas_call(
+    cells, grads = pl.pallas_call(
         functools.partial(kernel, factor),
         out_shape=[
-            jax.ShapeDtypeStruct((128, C), BF16),
-            jax.ShapeDtypeStruct((128, C), BF16),
-            jax.ShapeDtypeStruct((ROWS, C), F32),
-            jax.ShapeDtypeStruct((ROWS, C), F32),
+            jax.ShapeDtypeStruct((8, 2, 32, 128), BF16),
+            jax.ShapeDtypeStruct((2, 8 * SHARE, 16, 128), BF16),
         ],
         in_specs=[pl.BlockSpec(memory_space=pl.ANY)] * 4,
-        out_specs=[vmem] * 4,
+        out_specs=[pl.BlockSpec(memory_space=pl.ANY)] * 2,
         scratch_shapes=[
             scratch((128, C), BF16), scratch((128, C), BF16),
             scratch((2, ROWS, C), BF16), scratch((2, ROWS, C), BF16),
@@ -561,11 +583,11 @@
             scratch((2, 8 * SHARE, 16, 128), BF16),
             scratch((2, 8, SHARE, 16, 128), BF16),
             scratch((2, SHARE, 16, 128), F32), scratch((2, SHARE, 16, 128), F32),
-            scratch((2, 8 * SHARE, 16, 128), F32),
+            scratch((2, 8 * SHARE, 16, 128), BF16),
             scratch((8, 2, 32, 128), BF16), scratch((8, 2, 32, 128), BF16),
-            dma((4,)),
+            dma((4,)), dma((3,)),
             dma((2, 8)), dma((2, 8)), dma((4,)), dma((4,)),
-            dma((2, 2, 7)), dma((2, 2, 7)),
+            dma((2, 2, 9)), dma((2, 2, 9)),
             dma((2, 2, 4)), dma((2, 2, 4)),
             dma((4,)), dma((4,)), dma((2,)), dma((2,)),
             dma((2, 8)), dma((2, 8)), dma((2,)), dma((2,)), dma((2, 8)), dma((2, 8)),
@@ -578,6 +600,17 @@
         features.reshape(128, C), cotangent.reshape(128, C),
         weight_one.reshape(ROWS, C), weight_two.reshape(ROWS, C),
     )
+    out, gin, one, two = pl.pallas_call(
+        lay_out,
+        out_shape=[
+            jax.ShapeDtypeStruct((128, C), BF16),
+            jax.ShapeDtypeStruct((128, C), BF16),
+            jax.ShapeDtypeStruct((ROWS, C), F32),
+            jax.ShapeDtypeStruct((ROWS, C), F32),
+        ],
+        in_specs=[vmem] * 2,
+        out_specs=[vmem] * 4,
+    )(cells, grads)
     return out.reshape(shape), gin.reshape(shape), one.reshape(TAPS, 16, C), two.reshape(TAPS, 16, C)
 
 

time: 82.8 us -> 74.1 us (0.89); the launches traced: 82.6 us -> 72.6 us
  Pallas kernels: 77.2 us -> 72 us
  local copies, waits for them, and re-layouts: 4.76 us -> 0 us
    pallas_call x1, Pallas kernels: 77.2 us -> 69.9 us  [shards(): pl.pallas_call(functools.partial(kernel, factor), out_shape=[jax.ShapeDty...]
    unnamed x8 -> x0, local copies, waits for them, and re-layouts: 4.76 us -> none
    pallas_call x0 -> x1, Pallas kernels: none -> 2.12 us  [shards(): pl.pallas_call(lay_out, out_shape=[jax.ShapeDtypeStruct((128, C), BF16),...]
where the time goes in v3:
time: 74.1 us; the launch traced here: 72.6 us
  Pallas kernels  72 us (97%)
    pallas_call x1, Pallas kernels, shards(): pl.pallas_call(functools.partial(kernel, factor), out_shape=[jax.ShapeDty...  69.9 us
    pallas_call x1, Pallas kernels, shards(): pl.pallas_call(lay_out, out_shape=[jax.ShapeDtypeStruct((128, C), BF16),...  2.12 us

profile of v3, /device:TPU:24, one launch (start us, length us, event | category | flops | bytes accessed | tf_op | source)
XLA Modules:
  0.0 72.6 jit_solution(17636907664815708450)
XLA Ops:
  0.6 69.9 %shard_map.75 = (bf16[8,2,32,128]{3,2,1,0:T(8,128)(2,1)}, bf16[2,56,16,128]{3,2,1,0:T(8,128)(2,1)}) custom-call(bf16[128,256]{1,0:T(8,128)(2,1)} %bitcast.10, bf16[128,256]{1,0:T(8,128)(2,1)} %bitcast.11, bf16[432,256]{1,0:T(8,128)(2,1)} %bitcast.8, bf16[432,256]{1,0:T(8,128)(2,1)} %bitcast.9), custom_call_target="tpu_custom_call" | custom-call | tf_op jit(solution)/shard_map/pallas_call | solution.py:559
  70.5 2.1 %shard_map.76 = (bf16[128,256]{1,0:T(8,128)(2,1)}, bf16[128,256]{1,0:T(8,128)(2,1)}, f32[432,256]{1,0:T(8,128)}, f32[432,256]{1,0:T(8,128)}) custom-call(bf16[8,2,32,128]{3,2,1,0:T(8,128)(2,1)} %get-tuple-element.10.cells_ref, bf16[2,56,16,128]{3,2,1,0:T(8,128)(2,1)} %get-tuple-element.11.grads_ref), custom_call_target="tpu_custom_call" | custom-call | tf_op jit(solution)/shard_map/pallas_call | solution.py:603

commit v4 on v3

--- a/solution.py
+++ b/solution.py
@@ -92,8 +92,8 @@
                 total = term if total is None else total + term
         p_ref[:, at] = total[:16] + half_turn(total[16:32])
         lefts.append(total[32:])
-    hm_ref[...] = jnp.where(lo, lefts[0], half_turn(lefts[1]))
-    hp_ref[...] = jnp.where(lo, half_turn(lefts[0]), lefts[1])
+    hm_ref[...] = jnp.where(lo, lefts[0], half_turn(lefts[1])).astype(hm_ref.dtype)
+    hp_ref[...] = jnp.where(lo, half_turn(lefts[0]), lefts[1]).astype(hp_ref.dtype)
 
 
 def spread_halo(hp, hm, first, final):
@@ -131,7 +131,7 @@
     x_hbm, g_hbm, w1_hbm, w2_hbm,
     cells_hbm, grads_hbm,
     x_ref, g_ref, w1, w2,
-    ga, gb, z1, z2, r1, r2, f1, f2, y_ref, p_ref, hm, hp, rhm, rhp,
+    ga, gb, z1, z2, r1, r2, f1, f2, y_ref, p_ref, hm1, hp1, rhm1, rhp1, hm2, hp2, rhm2, rhp2,
     xm, xp, rxm, rxp, am, ap, ram, rap, imx, ima, gsum, gout, gin2, mine, sent, rr, part, other, full, oc, oall,
     in_sem, out_sem, w_send, w_recv, v_send, v_recv, a_send, a_recv,
     h_send, h_recv, n_send, n_recv, c_send, c_recv, r_send, r_recv, x_send, x_recv, f_send, f_recv, o_send, o_recv,
@@ -272,10 +272,12 @@
     wait_slices(0, r1, f1)
     cores(2, w2.at[1 - e], w2.at[1 - e]).wait_recv()
 
+    hm, hp, rhm, rhp = (hm1, hm2), (hp1, hp2), (rhm1, rhm2), (rhp1, rhp2)
+
     def halo_copies(phase, pair):
         return (
-            remote(hm.at[phase, pair], rhm.at[phase, pair], h_send.at[phase, 0, pair], h_recv.at[phase, 0, pair], d, below),
-            remote(hp.at[phase, pair], rhp.at[phase, pair], h_send.at[phase, 1, pair], h_recv.at[phase, 1, pair], d, above),
+            remote(hm[phase].at[pair], rhm[phase].at[pair], h_send.at[phase, 0, pair], h_recv.at[phase, 0, pair], d, below),
+            remote(hp[phase].at[pair], rhp[phase].at[pair], h_send.at[phase, 1, pair], h_recv.at[phase, 1, pair], d, above),
         )
 
     own_pair, other_pair = xl * 2 + y // 2, xl * 2 + 1 - y // 2
@@ -294,7 +296,7 @@
                 y = y_ref.at[2 * slot + t]
                 y[...] = dot(f[slot, :ROWS], v()) if t == 0 else dot(w[slot], g())
                 gather_taps(
-                    y, p_ref.at[t, pair, rows], hm.at[phase, pair, t, rows], hp.at[phase, pair, t, rows], 1 - 2 * t
+                    y, p_ref.at[t, pair, rows], hm[phase].at[pair, t, rows], hp[phase].at[pair, t, rows], 1 - 2 * t
                 )
         for copy in halo_copies(phase, pair):
             copy.start()
@@ -326,7 +328,7 @@
     each(4, x_edges)
 
     def halo_of(phase, t, pair):
-        return jnp.concatenate(spread_halo(rhp[phase, pair, t], rhm[phase, pair, t], first, final), axis=1)
+        return jnp.concatenate(spread_halo(rhp[phase][pair, t], rhm[phase][pair, t], first, final), axis=1)
 
     def middle(i):
         pair = pair_at(i)
@@ -391,7 +393,8 @@
             value = gsum[at] + gin2[(which, *at)]
             mine[which, tile] = value
             sent[which, tile] = value.astype(BF16)
-        each(8, lambda step: reduce_copy(which, step).start(), 1)
+        for step in (4, 3, 5, 2, 6, 1, 7):
+            reduce_copy(which, step).start()
 
     def pair_copy(which):
         return remote(part.at[which], other.at[which], x_send.at[which], x_recv.at[which], d, 2 * z + 1 - xh)
@@ -426,7 +429,7 @@
         spread_copy(which, 1).start()
 
     def spread_on(which):
-        for kind, then in ((0, (3, 2, 6)), (1, (5, 4, 7))):
+        for kind, then in ((0, (6, 3, 2)), (1, (7, 5, 4))):
             spread_copy(which, kind, True).wait_recv()
             for more in then:
                 spread_copy(which, more).start()
@@ -467,8 +470,8 @@
         convolve(1, pair, f2, lambda: gb[0, pair], w1, lambda: gb[1, pair])
 
     each(4, phase_two)
+    reduce_ring(0)
     spread(1)
-    reduce_ring(0)
 
     def home(to, source):
         return remote(oc.at[to], oall.at[source], o_send.at[to], o_recv.at[source], 2 * to + e, s)
@@ -574,7 +577,8 @@
             scratch((2, 512, C), BF16), scratch((2, 512, C), BF16),
             scratch((4, ROWS, C), F32),
             scratch((2, 4, 32, C), F32),
-            *[scratch((2, 4, 2, 32, 128), F32)] * 4,
+            *[scratch((4, 2, 32, 128), F32)] * 4,
+            *[scratch((4, 2, 32, 128), BF16)] * 4,
             *[scratch((4, 32, 128), BF16)] * 8,
             scratch((4, 2, ROWS, C), BF16), scratch((4, 2, ROWS, C), BF16),
             scratch((ROWS, C), F32),

time: 74.1 us -> 71.2 us (0.961); the launches traced: 72.6 us -> 70.5 us
  Pallas kernels: 72 us -> 69.9 us
    pallas_call x1, Pallas kernels: 69.9 us -> 67.8 us  [shards(): pl.pallas_call(functools.partial(kernel, factor), out_shape=[jax.ShapeDty...]
where the time goes in v4:
time: 71.2 us; the launch traced here: 70.5 us
  Pallas kernels  69.9 us (98%)
    pallas_call x1, Pallas kernels, shards(): pl.pallas_call(functools.partial(kernel, factor), out_shape=[jax.ShapeDty...  67.8 us
    pallas_call x1, Pallas kernels, shards(): pl.pallas_call(lay_out, out_shape=[jax.ShapeDtypeStruct((128, C), BF16),...  2.12 us

profile of v4, /device:TPU:24, one launch (start us, length us, event | category | flops | bytes accessed | tf_op | source)
XLA Modules:
  0.0 70.5 jit_solution(12536784230565589928)
XLA Ops:
  0.6 67.8 %shard_map.75 = (bf16[8,2,32,128]{3,2,1,0:T(8,128)(2,1)}, bf16[2,56,16,128]{3,2,1,0:T(8,128)(2,1)}) custom-call(bf16[128,256]{1,0:T(8,128)(2,1)} %bitcast.10, bf16[128,256]{1,0:T(8,128)(2,1)} %bitcast.11, bf16[432,256]{1,0:T(8,128)(2,1)} %bitcast.8, bf16[432,256]{1,0:T(8,128)(2,1)} %bitcast.9), custom_call_target="tpu_custom_call" | custom-call | tf_op jit(solution)/shard_map/pallas_call | solution.py:562
  68.4 2.1 %shard_map.76 = (bf16[128,256]{1,0:T(8,128)(2,1)}, bf16[128,256]{1,0:T(8,128)(2,1)}, f32[432,256]{1,0:T(8,128)}, f32[432,256]{1,0:T(8,128)}) custom-call(bf16[8,2,32,128]{3,2,1,0:T(8,128)(2,1)} %get-tuple-element.10.cells_ref, bf16[2,56,16,128]{3,2,1,0:T(8,128)(2,1)} %get-tuple-element.11.grads_ref), custom_call_target="tpu_custom_call" | custom-call | tf_op jit(solution)/shard_map/pallas_call | solution.py:607

commit v5 on v4

--- a/solution.py
+++ b/solution.py
@@ -231,7 +231,8 @@
         return remote(src, dst, v_send.at[index], v_recv.at[index], sibling, s)
 
     def send_slices(which, src, r):
-        each(8, lambda step: slices(which, src, r, lax.rem(m + step, 8), m).start(), 1)
+        for to in (XO, O, XU, XD, X, U, D):
+            slices(which, src, r, to, m).start()
         for slot in range(2):
             r[slot, m, e] = src[2 * m + slot]
 
@@ -466,7 +467,7 @@
         def _():
             reduce_ring(1)
 
-        pair = pair_at(i)
+        pair = pair_at(3 - i)
         convolve(1, pair, f2, lambda: gb[0, pair], w1, lambda: gb[1, pair])
 
     each(4, phase_two)
@@ -477,7 +478,7 @@
         return remote(oc.at[to], oall.at[source], o_send.at[to], o_recv.at[source], 2 * to + e, s)
 
     def finish(i):
-        pair = pair_at(i)
+        pair = pair_at(3 - i)
         for copy in halo_copies(1, pair):
             copy.wait_recv()
         for t in range(2):
@@ -495,6 +496,7 @@
     each(4, finish)
     spread(0)
     spread_on(1)
+    spread_on(0)
     oall[m] = oc[m]
 
     def wait_home(step):
@@ -503,7 +505,6 @@
 
     each(8, wait_home, 1)
     result(2).start()
-    spread_on(0)
     spread_end(1)
     spread_end(0)
     for which in range(3):

time: 71.2 us -> 70.9 us (level)
  no operation moved by 1% of the time
where the time goes in v5:
time: 70.9 us; the launch traced here: 70 us
  Pallas kernels  69.4 us (98%)
    pallas_call x1, Pallas kernels, shards(): pl.pallas_call(functools.partial(kernel, factor), out_shape=[jax.ShapeDty...  67.3 us
    pallas_call x1, Pallas kernels, shards(): pl.pallas_call(lay_out, out_shape=[jax.ShapeDtypeStruct((128, C), BF16),...  2.12 us

profile of v5, /device:TPU:24, one launch (start us, length us, event | category | flops | bytes accessed | tf_op | source)
XLA Modules:
  0.0 70.0 jit_solution(4293018919763714285)
XLA Ops:
  0.6 67.3 %shard_map.75 = (bf16[8,2,32,128]{3,2,1,0:T(8,128)(2,1)}, bf16[2,56,16,128]{3,2,1,0:T(8,128)(2,1)}) custom-call(bf16[128,256]{1,0:T(8,128)(2,1)} %bitcast.10, bf16[128,256]{1,0:T(8,128)(2,1)} %bitcast.11, bf16[432,256]{1,0:T(8,128)(2,1)} %bitcast.8, bf16[432,256]{1,0:T(8,128)(2,1)} %bitcast.9), custom_call_target="tpu_custom_call" | custom-call | tf_op jit(solution)/shard_map/pallas_call | solution.py:563
  67.9 2.1 %shard_map.76 = (bf16[128,256]{1,0:T(8,128)(2,1)}, bf16[128,256]{1,0:T(8,128)(2,1)}, f32[432,256]{1,0:T(8,128)}, f32[432,256]{1,0:T(8,128)}) custom-call(bf16[8,2,32,128]{3,2,1,0:T(8,128)(2,1)} %get-tuple-element.10.cells_ref, bf16[2,56,16,128]{3,2,1,0:T(8,128)(2,1)} %get-tuple-element.11.grads_ref), custom_call_target="tpu_custom_call" | custom-call | tf_op jit(solution)/shard_map/pallas_call | solution.py:608

commit v6 on v4

--- a/solution.py
+++ b/solution.py
@@ -325,7 +325,6 @@
         xm[pair] = lowest.astype(BF16)
         xp[pair] = highest.astype(BF16)
 
-    each(4, x_edges)
 
     def halo_of(phase, t, pair):
         return jnp.concatenate(spread_halo(rhp[phase][pair, t], rhm[phase][pair, t], first, final), axis=1)
@@ -340,15 +339,20 @@
         act = (pre * sig).astype(BF16)
         gb[0, pair, channels, :] = act
         gb[1, pair, channels, :] = (grad * sig * (1.0 + pre * (1.0 - sig))).astype(BF16)
-        lowest, highest = edge_planes(act.astype(F32))
+
+    each(4, middle)
+    depart(1, 1)
+
+    def act_edges(pair):
+        lowest, highest = edge_planes(gb[0, pair, channels, :].astype(F32))
         am[pair] = lowest.astype(BF16)
         ap[pair] = highest.astype(BF16)
 
-    each(4, middle)
-    depart(1, 1)
+    each(4, act_edges)
     near(2, am, ram, below).start()
     near(3, ap, rap, above).start()
     depart(1, 0)
+    each(4, x_edges)
     near(0, xm, rxm, below).start()
     near(1, xp, rxp, above).start()
 

time: 71.2 us -> 71 us (level)
  no operation moved by 1% of the time
where the time goes in v6:
time: 71 us; the launch traced here: 70 us
  Pallas kernels  69.4 us (98%)
    pallas_call x1, Pallas kernels, shards(): pl.pallas_call(functools.partial(kernel, factor), out_shape=[jax.ShapeDty...  67.3 us
    pallas_call x1, Pallas kernels, shards(): pl.pallas_call(lay_out, out_shape=[jax.ShapeDtypeStruct((128, C), BF16),...  2.12 us

profile of v6, /device:TPU:24, one launch (start us, length us, event | category | flops | bytes accessed | tf_op | source)
XLA Modules:
  0.0 70.0 jit_solution(8967691555286631649)
XLA Ops:
  0.6 67.3 %shard_map.75 = (bf16[8,2,32,128]{3,2,1,0:T(8,128)(2,1)}, bf16[2,56,16,128]{3,2,1,0:T(8,128)(2,1)}) custom-call(bf16[128,256]{1,0:T(8,128)(2,1)} %bitcast.10, bf16[128,256]{1,0:T(8,128)(2,1)} %bitcast.11, bf16[432,256]{1,0:T(8,128)(2,1)} %bitcast.8, bf16[432,256]{1,0:T(8,128)(2,1)} %bitcast.9), custom_call_target="tpu_custom_call" | custom-call | tf_op jit(solution)/shard_map/pallas_call | solution.py:566
  67.9 2.1 %shard_map.76 = (bf16[128,256]{1,0:T(8,128)(2,1)}, bf16[128,256]{1,0:T(8,128)(2,1)}, f32[432,256]{1,0:T(8,128)}, f32[432,256]{1,0:T(8,128)}) custom-call(bf16[8,2,32,128]{3,2,1,0:T(8,128)(2,1)} %get-tuple-element.10.cells_ref, bf16[2,56,16,128]{3,2,1,0:T(8,128)(2,1)} %get-tuple-element.11.grads_ref), custom_call_target="tpu_custom_call" | custom-call | tf_op jit(solution)/shard_map/pallas_call | solution.py:611
